TPU v7x, 256 devices: a whole 4x4x8 slice. The times are simulated.
256 devices in a mesh: replica: 8 (over z_lo, y), slab: 8 (over z_hi, core), heads: 4 (over x).
Axes of the slice: x: 4, y: 4, z: 8 (z_hi: 4, z_lo: 2; z = z_hi * 2 + z_lo), core: 2. Of those that a mesh axis runs over, the one named last changes fastest.
Arguments:
- q_video: bfloat16 [32768, 3072], P(('replica', 'slab', 'heads')), parts along dimension 0, may hold values from -6 to 6
- k_video: bfloat16 [32768, 3072], P(('replica', 'slab', 'heads')), parts along dimension 0, may hold values from -6 to 6
- v_video: bfloat16 [32768, 3072], P(('replica', 'slab', 'heads')), parts along dimension 0, may hold values from -6 to 6
- cot_video: bfloat16 [32768, 3072], P(('replica', 'slab', 'heads')), parts along dimension 0, may hold values from -6 to 6
- q_text: bfloat16 [2048, 3072], P(('replica', 'slab', 'heads')), parts along dimension 0, may hold values from -6 to 6
- k_text: bfloat16 [2048, 3072], P(('replica', 'slab', 'heads')), parts along dimension 0, may hold values from -6 to 6
- v_text: bfloat16 [2048, 3072], P(('replica', 'slab', 'heads')), parts along dimension 0, may hold values from -6 to 6
- cot_text: bfloat16 [2048, 3072], P(('replica', 'slab', 'heads')), parts along dimension 0, may hold values from -6 to 6
- gain_qv: float32 [1024], P('replica'), parts along dimension 0, may hold values from 0.5 to 5
- gain_kv: float32 [1024], P('replica'), parts along dimension 0, may hold values from 0.5 to 5
- gain_qt: float32 [1024], P('replica'), parts along dimension 0, may hold values from 0.5 to 5
- gain_kt: float32 [1024], P('replica'), parts along dimension 0, may hold values from 0.5 to 5
- windows: int32 [24, 3], replicated, may hold values from 1 to 3, as said below
- text_mask: int32 [2048], P('replica'), parts along dimension 0, may hold values from 0 to 1, as said below
Outputs:
- out_video: bfloat16 [32768, 3072], P(('replica', 'slab', 'heads')), parts along dimension 0
- out_text: bfloat16 [2048, 3072], P(('replica', 'slab', 'heads')), parts along dimension 0
- dq_video: bfloat16 [32768, 3072], P(('replica', 'slab', 'heads')), parts along dimension 0
- dk_video: bfloat16 [32768, 3072], P(('replica', 'slab', 'heads')), parts along dimension 0
- dv_video: bfloat16 [32768, 3072], P(('replica', 'slab', 'heads')), parts along dimension 0
- dq_text: bfloat16 [2048, 3072], P(('replica', 'slab', 'heads')), parts along dimension 0
- dk_text: bfloat16 [2048, 3072], P(('replica', 'slab', 'heads')), parts along dimension 0
- dv_text: bfloat16 [2048, 3072], P(('replica', 'slab', 'heads')), parts along dimension 0
- grad_gain_qv: float32 [1024], P('replica'), parts along dimension 0
- grad_gain_kv: float32 [1024], P('replica'), parts along dimension 0
- grad_gain_qt: float32 [1024], P('replica'), parts along dimension 0
- grad_gain_kt: float32 [1024], P('replica'), parts along dimension 0
There are 8 independent parts, one for each index of `replica`. A program takes and returns all parts, laid end to end along the dimension named above; an argument that names none is the same for every part. Nothing has to cross between parts.
Inputs may be any that keep to these rules, and one draw needn't show every extreme that they name: `windows`: every entry is 1 or 3; half of the heads have 3 along time. `text_mask`: A leading run of at least 64 ones, then zeros; the last entry is 0.
All inputs are finite; a program needn't handle non-finite values.
Results may differ from a plain program's by a relative error of at most 0.04.
The roundings to bfloat16 on the way count: a program that leaves them out, or rounds other values in their place, can miss the bound.
Values may be sent and summed in bfloat16 or wider, within the bound.
A program may use at most 192 MiB of HBM per device.

v0:
```python
import jax
import jax.numpy as jnp
from jax import lax
from jax.sharding import PartitionSpec as P

HEADS = 24
HD = 128
D = 3072
TEXT = 256
GRID_H = 16
GRID_W = 32


EPSILON = 1e-06
ROPE_BASE = 256.0
NEGATIVE = -1e30


def extended(cells, sides, width):
    for axis, dim in sides:
        count = lax.axis_size(axis)
        ends = count - 1
        head = lax.slice_in_dim(cells, 0, width, axis=dim)
        tail = lax.slice_in_dim(cells, cells.shape[dim] - width, cells.shape[dim], axis=dim)
        cells = jnp.concatenate(
            [
                lax.ppermute(tail, axis, [(i, (i + 1) % count) for i in range(ends)]),
                cells,
                lax.ppermute(head, axis, [((i + 1) % count, i) for i in range(ends)]),
            ],
            axis=dim,
        )
    return cells


def from_behind(block, axis, distance):
    devices = range(lax.axis_size(axis))
    route = [(i - distance, i) for i in devices if i - distance in devices]
    return lax.ppermute(block, axis, route)


def section_list(head_dim):
    first_len = head_dim // 8
    other_len = 7 * head_dim // 16
    return ((0, first_len), (first_len, other_len), (first_len + other_len, other_len))


def rope_tables(token_index, head_dim):
    frame_at = token_index // (GRID_H * GRID_W)
    height = token_index // GRID_W % GRID_H
    across = token_index % GRID_W
    places = (frame_at, height, across)
    angles = []
    for number, (start_offset, length) in enumerate(section_list(head_dim)):
        half_len = length // 2
        offsets = (jnp.arange(length, dtype=jnp.int32) % half_len).astype(jnp.float32)
        frequency = jnp.power(jnp.float32(ROPE_BASE), -2.0 * offsets / length)
        angles.append(places[number].astype(jnp.float32)[:, None] * frequency[None, :])
    angles = jnp.concatenate(angles, axis=1)
    return (jnp.cos(angles), jnp.sin(angles))


def swap_halves(values, head_dim):
    pieces = []
    for start_offset, length in section_list(head_dim):
        half_len = length // 2
        pieces.append(-values[..., start_offset + half_len : start_offset + length])
        pieces.append(values[..., start_offset : start_offset + half_len])
    return jnp.concatenate(pieces, axis=-1)


def rotate(values, cosine_tab, sine_tab, head_dim):
    return values * cosine_tab[:, None, :] + swap_halves(values, head_dim) * sine_tab[:, None, :]


def unit_rows(source, head_count):
    values = source.astype(jnp.float32).reshape(source.shape[0], head_count, HD)
    inverse = lax.rsqrt(jnp.mean(values * values, axis=-1, keepdims=True) + EPSILON)
    return (values * inverse, inverse)


def norm_back(grad_out, normed, inverse, gain):
    scaled = grad_out * gain
    grad_in = inverse * (scaled - normed * jnp.mean(scaled * normed, axis=-1, keepdims=True))
    return (grad_in, jnp.sum(grad_out * normed, axis=(0, 1)))


def matmul(first_op, second_op):
    return jnp.dot(first_op, second_op, preferred_element_type=jnp.float32)


def contract_last(first_op, second_op):
    return lax.dot_general(
        first_op, second_op, (((1,), (1,)), ((), ())), preferred_element_type=jnp.float32
    )


def contract_leading_axes(first_op, second_op):
    return lax.dot_general(
        first_op, second_op, (((0,), (0,)), ((), ())), preferred_element_type=jnp.float32
    )


def tile_places(band_token_count):
    per_frame = GRID_H * GRID_W
    query_pos = jnp.arange(band_token_count, dtype=jnp.int32)
    key_pos = jnp.arange(3 * band_token_count, dtype=jnp.int32)
    key_local = key_pos % band_token_count
    key_shift = key_pos // band_token_count - 1
    q_row = query_pos % per_frame // GRID_W // 8
    q_col = query_pos % GRID_W // 8
    k_row = key_local % per_frame // GRID_W // 8
    k_col = key_local % GRID_W // 8
    return (q_row, q_col, k_row, k_col, key_shift)


def window_mask(places, extent, slab_at, slab_total):
    q_row, q_col, k_row, k_col, key_shift = places
    exists = (slab_at + key_shift >= 0) & (slab_at + key_shift < slab_total)
    in_time = (jnp.abs(key_shift) <= extent[0] // 2) & exists
    rows_ok = jnp.abs(q_row[:, None] - k_row[None, :]) <= extent[1] // 2
    cols_ok = jnp.abs(q_col[:, None] - k_col[None, :]) <= extent[2] // 2
    return in_time[None, :] & rows_ok & cols_ok


def block_attend(
    queries, key_rows, value_rows, grad_rows, text_keys, text_values, allowed, usable, factor
):
    scores_video = jnp.where(allowed, contract_last(queries, key_rows) * factor, NEGATIVE)
    scores_text = jnp.where(usable[None, :], contract_last(queries, text_keys) * factor, NEGATIVE)
    row_top = jnp.maximum(jnp.max(scores_video, axis=1), jnp.max(scores_text, axis=1))[:, None]
    exp_video = jnp.exp(scores_video - row_top)
    exp_text = jnp.exp(scores_text - row_top)
    row_sum = (jnp.sum(exp_video, axis=1) + jnp.sum(exp_text, axis=1))[:, None]
    video_weight = exp_video.astype(jnp.bfloat16)
    weight_text = exp_text.astype(jnp.bfloat16)
    outputs = (
        (matmul(video_weight, value_rows) + matmul(weight_text, text_values)) / row_sum
    ).astype(jnp.bfloat16)
    row_dot = jnp.sum(
        grad_rows.astype(jnp.float32) * outputs.astype(jnp.float32), axis=1, keepdims=True
    )
    slope_video = (exp_video / row_sum * (contract_last(grad_rows, value_rows) - row_dot)).astype(
        jnp.bfloat16
    )
    slope_text = (exp_text / row_sum * (contract_last(grad_rows, text_values) - row_dot)).astype(
        jnp.bfloat16
    )
    query_gradient = factor * (matmul(slope_video, key_rows) + matmul(slope_text, text_keys))
    grad_k = factor * contract_leading_axes(slope_video, queries)
    value_gradient = contract_leading_axes(video_weight, grad_rows)
    text_key_gradient = factor * contract_leading_axes(slope_text, queries)
    text_value_gradient = contract_leading_axes(weight_text, grad_rows)
    return (outputs, query_gradient, grad_k, value_gradient, text_key_gradient, text_value_gradient)


def body(
    q_video,
    k_video,
    v_video,
    cot_video,
    q_text,
    k_text,
    v_text,
    cot_text,
    gain_qv,
    gain_kv,
    gain_qt,
    gain_kt,
    windows,
    text_mask,
):
    slab_total = lax.axis_size("slab")
    group_total = lax.axis_size("heads")
    slab_id = lax.axis_index("slab")
    group_id = lax.axis_index("heads")
    rows_dev = q_video.shape[0]
    text_dev = q_text.shape[0]
    band_token_count = rows_dev * group_total
    local_heads = HEADS // group_total
    group_width = local_heads * HD
    text_slab = TEXT // slab_total
    factor = HD ** (-0.5)
    token_index = (slab_id * group_total + group_id) * rows_dev + jnp.arange(
        rows_dev, dtype=jnp.int32
    )
    cosine_tab, sine_tab = rope_tables(token_index, HD)
    q_unit, q_inverse = unit_rows(q_video, HEADS)
    k_unit, k_inverse = unit_rows(k_video, HEADS)
    q_norm = (
        rotate(q_unit * gain_qv, cosine_tab, sine_tab, HD).astype(jnp.bfloat16).reshape(rows_dev, D)
    )
    k_norm = (
        rotate(k_unit * gain_kv, cosine_tab, sine_tab, HD).astype(jnp.bfloat16).reshape(rows_dev, D)
    )
    qt_unit, qt_inverse = unit_rows(q_text, HEADS)
    kt_unit, kt_inverse = unit_rows(k_text, HEADS)
    qt_norm = (qt_unit * gain_qt).astype(jnp.bfloat16).reshape(text_dev, D)
    kt_norm = (kt_unit * gain_kt).astype(jnp.bfloat16).reshape(text_dev, D)
    q_heads, k_heads, v_heads, g_heads = (
        lax.all_to_all(q_norm, "heads", split_axis=1, concat_axis=0, tiled=True),
        lax.all_to_all(k_norm, "heads", split_axis=1, concat_axis=0, tiled=True),
        lax.all_to_all(v_video, "heads", split_axis=1, concat_axis=0, tiled=True),
        lax.all_to_all(cot_video, "heads", split_axis=1, concat_axis=0, tiled=True),
    )
    gathered = (
        lax.all_gather(qt_norm, ("slab", "heads"), axis=0, tiled=True),
        lax.all_gather(kt_norm, ("slab", "heads"), axis=0, tiled=True),
        lax.all_gather(v_text, ("slab", "heads"), axis=0, tiled=True),
        lax.all_gather(cot_text, ("slab", "heads"), axis=0, tiled=True),
    )
    column_at = group_id * group_width
    qt_heads = lax.dynamic_slice_in_dim(gathered[0], column_at, group_width, 1)
    kt_heads = lax.dynamic_slice_in_dim(gathered[1], column_at, group_width, 1)
    vt_heads = lax.dynamic_slice_in_dim(gathered[2], column_at, group_width, 1)
    gt_heads = lax.dynamic_slice_in_dim(gathered[3], column_at, group_width, 1)
    key_pair = jnp.stack([k_heads, v_heads])
    widened = extended(key_pair, (("slab", 1),), band_token_count)
    k_wide = widened[0]
    v_wide = widened[1]
    usable = text_mask == 1
    keep_text = usable & (slab_id == 0)
    qt_three = qt_heads.reshape(TEXT, local_heads, HD)
    kt_three = kt_heads.reshape(TEXT, local_heads, HD)
    vt_three = vt_heads.reshape(TEXT, local_heads, HD)
    gt_three = gt_heads.reshape(TEXT, local_heads, HD)
    kn_three = k_heads.reshape(band_token_count, local_heads, HD)
    vn_three = v_heads.reshape(band_token_count, local_heads, HD)
    scores_tv = (
        jnp.einsum("qhd,khd->hqk", qt_three, kn_three, preferred_element_type=jnp.float32) * factor
    )
    scores_tt = jnp.where(
        keep_text[None, None, :],
        jnp.einsum("qhd,khd->hqk", qt_three, kt_three, preferred_element_type=jnp.float32) * factor,
        NEGATIVE,
    )
    local_top = jnp.maximum(jnp.max(scores_tv, axis=-1), jnp.max(scores_tt, axis=-1))
    row_top = lax.pmax(local_top, "slab")
    exp_tv = jnp.exp(scores_tv - row_top[..., None])
    exp_tt = jnp.exp(scores_tt - row_top[..., None])
    part_sum = jnp.sum(exp_tv, axis=-1) + jnp.sum(exp_tt, axis=-1)
    weight_tv = exp_tv.astype(jnp.bfloat16)
    weight_tt = exp_tt.astype(jnp.bfloat16)
    numer = jnp.einsum(
        "hqk,khd->qhd", weight_tv, vn_three, preferred_element_type=jnp.float32
    ) + jnp.einsum("hqk,khd->qhd", weight_tt, vt_three, preferred_element_type=jnp.float32)
    numer_all, row_sum = lax.psum((numer.reshape(TEXT, group_width), part_sum), "slab")
    out_text_three = (numer_all.reshape(TEXT, local_heads, HD) / row_sum.T[:, :, None]).astype(
        jnp.bfloat16
    )
    row_dot_text = jnp.sum(
        gt_three.astype(jnp.float32) * out_text_three.astype(jnp.float32), axis=-1
    ).T
    grad_tv = jnp.einsum("qhd,khd->hqk", gt_three, vn_three, preferred_element_type=jnp.float32)
    grad_tt = jnp.einsum("qhd,khd->hqk", gt_three, vt_three, preferred_element_type=jnp.float32)
    slope_tv = (exp_tv / row_sum[..., None] * (grad_tv - row_dot_text[..., None])).astype(
        jnp.bfloat16
    )
    slope_tt = (exp_tt / row_sum[..., None] * (grad_tt - row_dot_text[..., None])).astype(
        jnp.bfloat16
    )
    grad_qt_part = factor * (
        jnp.einsum("hqk,khd->qhd", slope_tv, kn_three, preferred_element_type=jnp.float32)
        + jnp.einsum("hqk,khd->qhd", slope_tt, kt_three, preferred_element_type=jnp.float32)
    )
    key_from_text = factor * jnp.einsum(
        "hqk,qhd->khd", slope_tv, qt_three, preferred_element_type=jnp.float32
    )
    value_from_text = jnp.einsum(
        "hqk,qhd->khd", weight_tv, gt_three, preferred_element_type=jnp.float32
    )
    text_key_self = factor * jnp.einsum(
        "hqk,qhd->khd", slope_tt, qt_three, preferred_element_type=jnp.float32
    )
    text_value_self = jnp.einsum(
        "hqk,qhd->khd", weight_tt, gt_three, preferred_element_type=jnp.float32
    )
    places = tile_places(band_token_count)
    reach_rows = lax.dynamic_slice_in_dim(windows, group_id * local_heads, local_heads, 0)

    def split_heads(source):
        return source.reshape(source.shape[0], local_heads, HD).transpose(1, 0, 2)

    def merge_heads(source):
        return source.transpose(1, 0, 2).reshape(source.shape[1], group_width)

    def per_head(packed):
        q_one, k_one, v_one, g_one, kt_one, vt_one, extent = packed
        allowed = window_mask(places, extent, slab_id, slab_total)
        return block_attend(q_one, k_one, v_one, g_one, kt_one, vt_one, allowed, usable, factor)

    mapped = lax.map(
        per_head,
        (
            split_heads(q_heads),
            split_heads(k_wide),
            split_heads(v_wide),
            split_heads(g_heads),
            split_heads(kt_heads),
            split_heads(vt_heads),
            reach_rows,
        ),
    )
    out_heads = merge_heads(mapped[0])
    query_gradient = merge_heads(mapped[1])
    grad_kwide = merge_heads(mapped[2])
    grad_vwide = merge_heads(mapped[3])
    text_key_gradient = merge_heads(mapped[4])
    text_value_gradient = merge_heads(mapped[5])
    low_pack = jnp.stack([grad_kwide[:band_token_count], grad_vwide[:band_token_count]])
    high_pack = jnp.stack([grad_kwide[2 * band_token_count :], grad_vwide[2 * band_token_count :]])
    from_above = from_behind(low_pack.astype(jnp.bfloat16), "slab", -1).astype(low_pack.dtype)
    from_below = from_behind(high_pack.astype(jnp.bfloat16), "slab", 1).astype(high_pack.dtype)
    grad_k_local = (
        grad_kwide[band_token_count : 2 * band_token_count]
        + key_from_text.reshape(band_token_count, group_width)
        + from_above[0]
        + from_below[0]
    )
    grad_v_local = (
        grad_vwide[band_token_count : 2 * band_token_count]
        + value_from_text.reshape(band_token_count, group_width)
        + from_above[1]
        + from_below[1]
    )
    out_video, dq_rows, dk_rows, dv_video = (
        lax.all_to_all(out_heads, "heads", split_axis=0, concat_axis=1, tiled=True),
        lax.all_to_all(
            query_gradient.astype(jnp.bfloat16), "heads", split_axis=0, concat_axis=1, tiled=True
        ),
        lax.all_to_all(
            grad_k_local.astype(jnp.bfloat16), "heads", split_axis=0, concat_axis=1, tiled=True
        ),
        lax.all_to_all(
            grad_v_local.astype(jnp.bfloat16), "heads", split_axis=0, concat_axis=1, tiled=True
        ),
    )
    out_text_rows = lax.dynamic_slice_in_dim(
        out_text_three.reshape(TEXT, group_width), slab_id * text_slab, text_slab, 0
    )
    out_text = lax.all_to_all(out_text_rows, "heads", split_axis=0, concat_axis=1, tiled=True)
    grad_qt_flat = grad_qt_part.reshape(TEXT, group_width)
    grad_kt_all = text_key_gradient + text_key_self.reshape(TEXT, group_width)
    grad_vt_all = text_value_gradient + text_value_self.reshape(TEXT, group_width)
    summed_q, summed_k, summed_v = (
        lax.psum_scatter(
            grad_qt_flat.astype(jnp.bfloat16), "slab", scatter_dimension=0, tiled=True
        ).astype(jnp.float32),
        lax.psum_scatter(
            grad_kt_all.astype(jnp.bfloat16), "slab", scatter_dimension=0, tiled=True
        ).astype(jnp.float32),
        lax.psum_scatter(
            grad_vt_all.astype(jnp.bfloat16), "slab", scatter_dimension=0, tiled=True
        ).astype(jnp.float32),
    )
    dqt_rows, dkt_rows, dv_text = (
        lax.all_to_all(
            summed_q.astype(jnp.bfloat16), "heads", split_axis=0, concat_axis=1, tiled=True
        ),
        lax.all_to_all(
            summed_k.astype(jnp.bfloat16), "heads", split_axis=0, concat_axis=1, tiled=True
        ),
        lax.all_to_all(
            summed_v.astype(jnp.bfloat16), "heads", split_axis=0, concat_axis=1, tiled=True
        ),
    )

    def heads_view(source):
        return source.astype(jnp.float32).reshape(source.shape[0], HEADS, HD)

    dq_in, part_qv = norm_back(
        rotate(heads_view(dq_rows), cosine_tab, -sine_tab, HD), q_unit, q_inverse, gain_qv
    )
    dk_in, part_kv = norm_back(
        rotate(heads_view(dk_rows), cosine_tab, -sine_tab, HD), k_unit, k_inverse, gain_kv
    )
    dqt_in, part_qt = norm_back(heads_view(dqt_rows), qt_unit, qt_inverse, gain_qt)
    dkt_in, part_kt = norm_back(heads_view(dkt_rows), kt_unit, kt_inverse, gain_kt)
    gain_total = lax.psum(jnp.stack([part_qv, part_kv, part_qt, part_kt]), ("slab", "heads"))
    dq_video = dq_in.reshape(rows_dev, D).astype(jnp.bfloat16)
    dk_video = dk_in.reshape(rows_dev, D).astype(jnp.bfloat16)
    dq_text = dqt_in.reshape(text_dev, D).astype(jnp.bfloat16)
    dk_text = dkt_in.reshape(text_dev, D).astype(jnp.bfloat16)
    return (
        out_video,
        out_text,
        dq_video,
        dk_video,
        dv_video,
        dq_text,
        dk_text,
        dv_text,
        gain_total[0],
        gain_total[1],
        gain_total[2],
        gain_total[3],
    )


def solution(mesh):
    placed = (
        P(("replica", "slab", "heads"), None),
        P(("replica", "slab", "heads"), None),
        P(("replica", "slab", "heads"), None),
        P(("replica", "slab", "heads"), None),
        P(("replica", "slab", "heads"), None),
        P(("replica", "slab", "heads"), None),
        P(("replica", "slab", "heads"), None),
        P(("replica", "slab", "heads"), None),
        P("replica"),
        P("replica"),
        P("replica"),
        P("replica"),
        P(),
        P("replica"),
    )
    return jax.shard_map(
        body,
        mesh=mesh,
        in_specs=placed,
        out_specs=(
            P(("replica", "slab", "heads"), None),
            P(("replica", "slab", "heads"), None),
            P(("replica", "slab", "heads"), None),
            P(("replica", "slab", "heads"), None),
            P(("replica", "slab", "heads"), None),
            P(("replica", "slab", "heads"), None),
            P(("replica", "slab", "heads"), None),
            P(("replica", "slab", "heads"), None),
            P("replica"),
            P("replica"),
            P("replica"),
            P("replica"),
        ),
        check_vma=False,
    )
```

profile of v0, /device:TPU:1, one launch (start us, length us, event | category | flops | bytes accessed | tf_op | source)
XLA Modules:
  0.0 909.3 jit_solution(6624496047617595224)
XLA Ops:
  25.5 13.1 %concatenate.30 = f32[128,24,128]{0,2,1:T(8,128)} concatenate(f32[128,24,8]{0,2,1:T(8,128)} %get-tuple-element.675, f32[128,24,8]{0,2,1:T(8,128)} %get-tuple-element.674, f32[128,24,28]{0,2,1:T(8,128)} %get-tuple-element.673, f32[128,24,28]{0,2,1:T(8,128)} %get-tuple-element.672, f32[128,24,28]{0,2,1:T(8,128)} %get-tuple-element.671, f32[128,24,28]{0,2,1:T(8,128)} %get-tuple-element.670), dimensions={2} | concatenate | bytes 3145728 | tf_op jit(solution)/shard_map/concatenate | solution.py:69
  40.3 12.8 %concatenate.31 = f32[128,24,128]{0,2,1:T(8,128)} concatenate(f32[128,24,8]{0,2,1:T(8,128)} %get-tuple-element.669, f32[128,24,8]{0,2,1:T(8,128)} %get-tuple-element.668, f32[128,24,28]{0,2,1:T(8,128)} %get-tuple-element.667, f32[128,24,28]{0,2,1:T(8,128)} %get-tuple-element.666, f32[128,24,28]{0,2,1:T(8,128)} %get-tuple-element.665, f32[128,24,28]{0,2,1:T(8,128)S(1)} %get-tuple-element.664), dimensions={2} | concatenate | bytes 3145728 | tf_op jit(solution)/shard_map/concatenate | solution.py:69
  59.7 5.0 all-to-all-start.1
  65.8 8.9 all-to-all-done.1
  74.7 4.2 all-to-all-start.2
  79.8 8.6 all-to-all-done.2
  91.2 10.7 %collective-permute-start = (bf16[2,512,768]{2,1,0:T(8,128)(2,1)}, bf16[2,512,768]{2,1,0:T(8,128)(2,1)}, u32[]{:S(2)}, u32[]{:S(2)}) collective-permute-start(bf16[2,512,768]{2,1,0:T(8,128)(2,1)} %pad_maximum_fusion.1), channel_id=1, source_target_pairs={{0,4},{4,8},{8,12},{12,16},{16,20},{20,24},{24,28},{1,5},{5,9},{9,... | collective-permute-start | bytes 4718600 | tf_op jit(solution)/shard_map/ppermute | solution.py:27
  104.0 3.5 all-to-all-start
  108.7 8.7 all-to-all-done
  117.4 4.7 all-to-all-start.3
  142.3 5.9 collective-permute-done.1
  152.0 4.3 copy.515
  160.9 45.1 %all-gather.9.cloned.1.call-done = bf16[256,3072]{1,0:T(8,128)(2,1)} async-done(((bf16[8,3072]{1,0:T(8,128)(2,1)}), bf16[256,3072]{1,0:T(8,128)(2,1)}) %all-gather.9.cloned.1.call-update) | async-done | bytes 1572880 | tf_op jit(solution)/shard_map/all_gather | solution.py:207
  206.0 52.7 %all-gather.7.cloned.1.call-done = bf16[256,3072]{1,0:T(8,128)(2,1)} async-done(((bf16[8,3072]{1,0:T(8,128)(2,1)}), bf16[256,3072]{1,0:T(8,128)(2,1)}) %all-gather.7.cloned.1.call-update) | async-done | bytes 1572880 | tf_op jit(solution)/shard_map/all_gather | solution.py:209
  261.6 234.3 %while.24 = (s32[]{:T(128)}, bf16[6,512,128]{1,2,0:T(8,128)(2,1)}, bf16[6,512,128]{2,1,0:T(8,128)(2,1)}, f32[6,1536,128]{1,2,0:T(8,128)}, f32[6,1536,128]{1,2,0:...) while((s32[]{:T(128)}, bf16[6,512,128]{1,2,0:T(8,128)(2,1)}, ...), condition=%wide.region_9.10_spmd.clone, body=%wide.region_3.9_spmd.clone.sunk | while | flops 1429415424 | bytes 53088532 | solution.py:292
  270.8 3.1 fusion.278
  309.7 3.1 fusion.278
  348.7 3.1 fusion.278
  387.7 3.1 fusion.278
  426.8 3.1 fusion.278
  465.8 3.1 fusion.278
  498.6 4.2 all-to-all-start.6
  518.5 40.2 %pmax.7 = f32[6,256]{1,0:T(8,128)} all-reduce(f32[6,256]{1,0:T(8,128)} %max.16), channel_id=1, replica_groups=mesh['replica'=8,'slab'=8,'heads'=4] {'slab'}, use_global_device_ids=true, to_apply=%region_13.14 | all-reduce | flops 1536 | bytes 12288 | tf_op jit(solution)/shard_map/pmax | solution.py:238
  571.5 5.1 collective-permute-start.3
  585.8 3.5 slice_add_fusion
  589.2 4.2 all-to-all-start.4
  601.8 15.1 %psum.22 = f32[6,256]{1,0:T(8,128)} all-reduce(f32[6,256]{1,0:T(8,128)} %add.329), channel_id=1, replica_groups=mesh['replica'=8,'slab'=8,'heads'=4] {'slab'}, use_global_device_ids=true, to_apply=%region_17.18 | all-reduce | flops 1536 | bytes 12288 | tf_op jit(solution)/shard_map/psum | solution.py:247
  625.2 13.2 %concatenate.33 = f32[128,24,128]{0,2,1:T(8,128)} concatenate(f32[128,24,8]{0,2,1:T(8,128)} %get-tuple-element.657, f32[128,24,8]{0,2,1:T(8,128)} %get-tuple-element.656, f32[128,24,28]{0,2,1:T(8,128)} %get-tuple-element.655, f32[128,24,28]{0,2,1:T(8,128)} %get-tuple-element.654, f32[128,24,28]{0,2,1:T(8,128)} %get-tuple-element.653, f32[128,24,28]{0,2,1:T(8,128)} %get-tuple-element.652), dimensions={2} | concatenate | bytes 3145728 | tf_op jit(solution)/shard_map/concatenate | solution.py:69
  638.4 12.5 %all-reduce.2.cloned.1.call-done = f32[256,768]{0,1:T(8,128)} async-done(((f32[256,768]{0,1:T(8,128)}), f32[256,768]{0,1:T(8,128)}) %all-reduce.2.cloned.1.call-update) | async-done | bytes 786448 | tf_op jit(solution)/shard_map/psum | solution.py:247
  652.4 3.8 multiply_convert_fusion
  662.0 26.6 %reduce-scatter.8.cloned.1.call-done = bf16[32,768]{1,0:T(8,128)(2,1)} async-done(((bf16[256,768]{1,0:T(8,128)(2,1)}), bf16[32,768]{1,0:T(8,128)(2,1)}) %reduce-scatter.8.cloned.1.call-update) | async-done | bytes 49168 | tf_op jit(solution)/shard_map/reduce_scatter | solution.py:352
  688.6 3.9 all-to-all-start.11
  697.0 3.9 all-to-all-start.5
  705.4 20.9 %reduce-scatter.6.cloned.1.call-done = bf16[32,768]{1,0:T(8,128)(2,1)} async-done(((bf16[256,768]{1,0:T(8,128)(2,1)}), bf16[32,768]{1,0:T(8,128)(2,1)}) %reduce-scatter.6.cloned.1.call-update) | async-done | bytes 49168 | tf_op jit(solution)/shard_map/reduce_scatter | solution.py:349
  726.3 4.0 all-to-all-start.10
  733.1 3.2 fusion.190
  739.8 3.3 add_convert_fusion
  744.3 20.5 %reduce-scatter.4.cloned.1.call-done = bf16[32,768]{1,0:T(8,128)(2,1)} async-done(((bf16[256,768]{1,0:T(8,128)(2,1)}), bf16[32,768]{1,0:T(8,128)(2,1)}) %reduce-scatter.4.cloned.1.call-update) | async-done | bytes 49168 | tf_op jit(solution)/shard_map/reduce_scatter | solution.py:346
  764.8 3.9 all-to-all-start.9
  768.8 4.2 all-to-all-done.9
  773.1 3.5 all-to-all-start.7
  779.5 5.4 all-to-all-done.7
  784.9 4.2 all-to-all-start.8
  791.4 11.3 %concatenate.34 = f32[128,24,128]{0,2,1:T(8,128)} concatenate(f32[128,24,8]{0,2,1:T(8,128)S(1)} %get-tuple-element.663, f32[128,24,8]{0,2,1:T(8,128)S(1)} %get-tuple-element.662, f32[128,24,28]{0,2,1:T(8,128)} %get-tuple-element.661, f32[128,24,28]{0,2,1:T(8,128)} %get-tuple-element.660, f32[128,24,28]{0,2,1:T(8,128)} %get-tuple-element.659, f32[128,24,28]{0,2,1:T(8,128)} %get-tuple-element.658), dimensions={2} | concatenate | bytes 3145728 | tf_op jit(solution)/shard_map/concatenate | solution.py:69
  802.8 5.4 multiply_reduce_fusion.3
  813.8 3.4 multiply_reduce_fusion.2
  817.3 71.1 %psum.23 = f32[4,128]{1,0:T(4,128)S(1)} all-reduce(f32[4,128]{1,0:T(4,128)S(1)} %pad_maximum_fusion.5), channel_id=1, replica_groups=mesh['replica'=8,'slab'=8,'heads'=4] {'slab','heads'}, use_global_device_ids=true, to_apply=%region_34.35 | all-reduce | flops 512 | bytes 4096 | tf_op jit(solution)/shard_map/psum | solution.py:379
  891.3 4.4 fusion.122
  (672 shorter events, 334.0 us)
Async XLA Ops:
  7.2 124.5 %copy-start = (s32[24,3]{0,1:T(4,128)S(1)}, s32[24,3]{0,1:T(4,128)}, u32[]{:S(2)}) copy-start(s32[24,3]{0,1:T(4,128)} %param.28) | copy-start | bytes 868
  7.2 151.6 %all-gather.5.cloned.1.call-start = ((), (), s32[]{:S(2)}) async-start(), calls=%async_computation.15 | async-start | bytes 1622016 | tf_op jit(solution)/shard_map/all_gather | solution.py:208
  12.2 146.6 %all-gather.11.cloned.1.call-start = ((), (), s32[]{:S(2)}) async-start(), calls=%async_computation.19 | async-start | bytes 1622016 | tf_op jit(solution)/shard_map/all_gather | solution.py:210
  13.0 193.0 %all-gather.9.cloned.1.call-start = ((), (), s32[]{:S(2)}) async-start(), calls=%async_computation.17 | async-start | bytes 1622016 | tf_op jit(solution)/shard_map/all_gather | solution.py:207
  18.2 38.9 %copy-start.20 = (bf16[128,3072]{0,1:T(8,128)(2,1)}, bf16[128,3072]{0,1:T(8,128)(2,1)S(1)}, u32[]{:S(2)}) copy-start(bf16[128,3072]{0,1:T(8,128)(2,1)S(1)} %copy.511) | copy-start | bytes 2359300
  18.3 110.0 %copy-start.7 = (f32[128,3072]{0,1:T(8,128)}, f32[128,3072]{0,1:T(8,128)S(1)}, u32[]{:S(2)}) copy-start(f32[128,3072]{0,1:T(8,128)S(1)} %convert_element_type.295) | copy-start | bytes 4718596
  20.6 36.5 %copy-start.21 = (bf16[128,3072]{0,1:T(8,128)(2,1)}, bf16[128,3072]{0,1:T(8,128)(2,1)S(1)}, u32[]{:S(2)}) copy-start(bf16[128,3072]{0,1:T(8,128)(2,1)S(1)} %copy.509) | copy-start | bytes 2359300
  54.1 68.1 %copy-start.47 = (f32[128,128]{0,1:T(8,128)}, f32[128,128]{0,1:T(8,128)S(1)}, u32[]{:S(2)}) copy-start(f32[128,128]{0,1:T(8,128)S(1)} %get-tuple-element.680) | copy-start | bytes 196612
  59.7 15.1 %all-to-all-start.1 = ((bf16[128,4,768]{0,2,1:T(8,128)(2,1)}), bf16[128,4,768]{0,2,1:T(8,128)(2,1)S(1)}, u32[]{:S(2)}, u32[]{:S(2)}) async-start(bf16[128,4,768]{0,2,1:T(8,128)(2,1)} %bitcast.520), calls=%async_computation.1 | async-start | bytes 1572864 | tf_op jit(solution)/shard_map/all_to_all | solution.py:202
  74.7 13.7 %all-to-all-start.2 = ((bf16[128,4,768]{0,2,1:T(8,128)(2,1)}), bf16[128,4,768]{0,2,1:T(8,128)(2,1)}, u32[]{:S(2)}, u32[]{:S(2)}) async-start(bf16[128,4,768]{0,2,1:T(8,128)(2,1)} %bitcast.15), calls=%async_computation.2 | async-start | bytes 1572864 | tf_op jit(solution)/shard_map/all_to_all | solution.py:203
  78.9 179.8 %all-gather.7.cloned.1.call-start = ((), (), s32[]{:S(2)}) async-start(), calls=%async_computation.16 | async-start | bytes 1622016 | tf_op jit(solution)/shard_map/all_gather | solution.py:209
  79.8 11.4 %copy-start.26 = (bf16[4,128,768]{2,1,0:T(8,128)(2,1)}, bf16[4,128,768]{2,1,0:T(8,128)(2,1)S(1)}, u32[]{:S(2)}) copy-start(bf16[4,128,768]{2,1,0:T(8,128)(2,1)S(1)} %copy.512) | copy-start | bytes 2359300
  91.2 51.1 %collective-permute-start = (bf16[2,512,768]{2,1,0:T(8,128)(2,1)}, bf16[2,512,768]{2,1,0:T(8,128)(2,1)}, u32[]{:S(2)}, u32[]{:S(2)}) collective-permute-start(bf16[2,512,768]{2,1,0:T(8,128)(2,1)} %pad_maximum_fusion.1), channel_id=1, source_target_pairs={{0,4},{4,8},{8,12},{12,16},{16,20},{20,24},{24,28},{1,5},{5,9},{9,... | collective-permute-start | bytes 4718600 | tf_op jit(solution)/shard_map/ppermute | solution.py:27
  101.9 46.3 %collective-permute-start.1 = (bf16[2,512,768]{2,1,0:T(8,128)(2,1)}, bf16[2,512,768]{2,1,0:T(8,128)(2,1)}, u32[]{:S(2)}, u32[]{:S(2)}) collective-permute-start(bf16[2,512,768]{2,1,0:T(8,128)(2,1)} %pad_maximum_fusion.1), channel_id=1, source_target_pairs={{4,0},{8,4},{12,8},{16,12},{20,16},{24,20},{28,24},{5,1},{9,5},{13... | collective-permute-start | bytes 4718600 | tf_op jit(solution)/shard_map/ppermute | solution.py:29
  104.0 13.4 %all-to-all-start = ((bf16[128,4,768]{0,2,1:T(8,128)(2,1)}), bf16[128,4,768]{0,2,1:T(8,128)(2,1)S(1)}, u32[]{:S(2)}, u32[]{:S(2)}) async-start(bf16[128,4,768]{0,2,1:T(8,128)(2,1)} %bitcast.519), calls=%async_computation | async-start | bytes 1572864 | tf_op jit(solution)/shard_map/all_to_all | solution.py:201
  117.4 19.6 %all-to-all-start.3 = ((bf16[128,4,768]{0,2,1:T(8,128)(2,1)}), bf16[128,4,768]{0,2,1:T(8,128)(2,1)}, u32[]{:S(2)}, u32[]{:S(2)}) async-start(bf16[128,4,768]{0,2,1:T(8,128)(2,1)} %bitcast.27), calls=%async_computation.3 | async-start | bytes 1572864 | tf_op jit(solution)/shard_map/all_to_all | solution.py:204
  160.7 100.9 %copy-start.85 = (s32[6,3]{0,1:T(4,128)S(1)}, s32[6,3]{0,1:T(4,128)}, u32[]{:S(2)}) copy-start(s32[6,3]{0,1:T(4,128)} %constant_dynamic-slice_fusion.5) | copy-start | bytes 220
  498.6 90.6 %all-to-all-start.6 = ((bf16[4,128,768]{1,2,0:T(8,128)(2,1)}), bf16[4,128,768]{1,2,0:T(8,128)(2,1)}, u32[]{:S(2)}, u32[]{:S(2)}) async-start(bf16[4,128,768]{1,2,0:T(8,128)(2,1)} %copy.542), calls=%async_computation.6 | async-start | bytes 1572864 | tf_op jit(solution)/shard_map/all_to_all | solution.py:328
  502.8 148.1 %all-reduce.2.cloned.1.call-start = ((), (), s32[]{:S(2)}) async-start(), calls=%async_computation.18 | async-start | bytes 1572864 | tf_op jit(solution)/shard_map/psum | solution.py:247
  512.0 218.2 %collective-permute-start.2 = (bf16[2,512,768]{2,1,0:T(8,128)(2,1)}, bf16[2,512,768]{2,1,0:T(8,128)(2,1)}, u32[]{:S(2)}, u32[]{:S(2)}) collective-permute-start(bf16[2,512,768]{2,1,0:T(8,128)(2,1)} %pad_maximum_fusion.2), channel_id=1, source_target_pairs={{4,0},{8,4},{12,8},{16,12},{20,16},{24,20},{28,24},{5,1},{9,5},{13... | collective-permute-start | bytes 4718600 | tf_op jit(solution)/shard_map/ppermute | solution.py:39
  571.5 161.6 %collective-permute-start.3 = (bf16[2,512,768]{2,1,0:T(8,128)(2,1)}, bf16[2,512,768]{2,1,0:T(8,128)(2,1)}, u32[]{:S(2)}, u32[]{:S(2)}) collective-permute-start(bf16[2,512,768]{2,1,0:T(8,128)(2,1)} %pad_maximum_fusion.3), channel_id=1, source_target_pairs={{0,4},{4,8},{8,12},{12,16},{16,20},{20,24},{24,28},{1,5},{5,9},{9,... | collective-permute-start | bytes 4718600 | tf_op jit(solution)/shard_map/ppermute | solution.py:39
  589.2 31.4 %all-to-all-start.4 = ((bf16[4,128,768]{2,1,0:T(8,128)(2,1)}), bf16[4,128,768]{2,1,0:T(8,128)(2,1)}, u32[]{:S(2)}, u32[]{:S(2)}) async-start(bf16[4,128,768]{2,1,0:T(8,128)(2,1)} %copy.528), calls=%async_computation.4 | async-start | bytes 1572864 | tf_op jit(solution)/shard_map/all_to_all | solution.py:327
  593.4 95.2 %reduce-scatter.8.cloned.1.call-start = ((), (), s32[]{:S(2)}) async-start(), calls=%async_computation.22 | async-start | bytes 442368 | tf_op jit(solution)/shard_map/reduce_scatter | solution.py:352
  601.7 124.6 %reduce-scatter.6.cloned.1.call-start = ((), (), s32[]{:S(2)}) async-start(), calls=%async_computation.21 | async-start | bytes 442368 | tf_op jit(solution)/shard_map/reduce_scatter | solution.py:349
  688.6 8.4 all-to-all-start.11
  697.0 8.4 all-to-all-start.5
  700.9 63.9 %reduce-scatter.4.cloned.1.call-start = ((), (), s32[]{:S(2)}) async-start(), calls=%async_computation.20 | async-start | bytes 442368 | tf_op jit(solution)/shard_map/reduce_scatter | solution.py:346
  726.3 38.5 %all-to-all-start.10 = ((bf16[4,8,768]{2,1,0:T(8,128)(2,1)}), bf16[4,8,768]{2,1,0:T(8,128)(2,1)S(1)}, u32[]{:S(2)}, u32[]{:S(2)}) async-start(bf16[4,8,768]{2,1,0:T(8,128)(2,1)} %bitcast.543), calls=%async_computation.12 | async-start | bytes 98304 | tf_op jit(solution)/shard_map/all_to_all | solution.py:360
  743.1 25.6 %copy-start.63 = (bf16[8,3072]{1,0:T(8,128)(2,1)S(1)}, bf16[8,3072]{1,0:T(8,128)(2,1)}, u32[]{:S(2)}) copy-start(bf16[8,3072]{1,0:T(8,128)(2,1)} %param.21) | copy-start | bytes 147460
  743.1 25.6 %copy-start.73 = (f32[8,4,768]{2,1,0:T(4,128)S(1)}, f32[8,4,768]{2,1,0:T(4,128)}, u32[]{:S(2)}) copy-start(f32[8,4,768]{2,1,0:T(4,128)} %mul.676) | copy-start | bytes 294916
  744.3 32.3 %copy-start.64 = (bf16[8,3072]{1,0:T(8,128)(2,1)S(1)}, bf16[8,3072]{1,0:T(8,128)(2,1)}, u32[]{:S(2)}) copy-start(bf16[8,3072]{1,0:T(8,128)(2,1)} %param.20) | copy-start | bytes 147460
  744.3 32.3 %copy-start.72 = (f32[8,4,768]{2,1,0:T(4,128)S(1)}, f32[8,4,768]{2,1,0:T(4,128)}, u32[]{:S(2)}) copy-start(f32[8,4,768]{2,1,0:T(4,128)} %mul.673) | copy-start | bytes 294916
  744.3 33.1 %copy-start.57 = (f32[1,8,24,128]{3,1,2,0:T(8,128)S(1)}, f32[1,8,24,128]{3,1,2,0:T(8,128)}, u32[]{:S(2)}) copy-start(f32[1,8,24,128]{3,1,2,0:T(8,128)} %copy-done.56) | copy-start | bytes 294916
  744.3 33.1 %copy-start.89 = (f32[8,24]{1,0:T(8,128)S(1)}, f32[8,24]{1,0:T(8,128)}, u32[]{:S(2)}) copy-start(f32[8,24]{1,0:T(8,128)} %copy-done.87) | copy-start | bytes 2308
  744.3 33.1 %copy-start.102 = (f32[128]{0:T(128)S(1)}, f32[128]{0:T(128)}, u32[]{:S(2)}) copy-start(f32[128]{0:T(128)} %param.27) | copy-start | bytes 1540
  764.8 8.2 all-to-all-start.9
  773.1 11.8 %all-to-all-start.7 = ((bf16[4,128,768]{2,1,0:T(8,128)(2,1)}), bf16[4,128,768]{2,1,0:T(8,128)(2,1)S(1)}, u32[]{:S(2)}, u32[]{:S(2)}) async-start(bf16[4,128,768]{2,1,0:T(8,128)(2,1)} %add_convert_fusion), calls=%async_computation.7 | async-start | bytes 1572864 | tf_op jit(solution)/shard_map/all_to_all | solution.py:331
  784.9 104.0 %all-to-all-start.8 = ((bf16[4,128,768]{1,2,0:T(8,128)(2,1)}), bf16[4,128,768]{1,2,0:T(8,128)(2,1)}, u32[]{:S(2)}, u32[]{:S(2)}) async-start(bf16[4,128,768]{1,2,0:T(8,128)(2,1)} %fusion.136), calls=%async_computation.8 | async-start | bytes 1572864 | tf_op jit(solution)/shard_map/all_to_all | solution.py:334
  791.4 11.4 %copy-start.8 = (f32[128,3072]{0,1:T(8,128)S(1)}, f32[128,3072]{0,1:T(8,128)}, u32[]{:S(2)}) copy-start(f32[128,3072]{0,1:T(8,128)} %copy-done.7) | copy-start | bytes 4718596
  791.4 11.4 %copy-start.10 = (f32[128,3072]{0,1:T(8,128)S(1)}, f32[128,3072]{0,1:T(8,128)}, u32[]{:S(2)}) copy-start(f32[128,3072]{0,1:T(8,128)} %copy-done.9) | copy-start | bytes 4718596
  791.4 11.4 %copy-start.48 = (f32[128,128]{0,1:T(8,128)S(1)}, f32[128,128]{0,1:T(8,128)}, u32[]{:S(2)}) copy-start(f32[128,128]{0,1:T(8,128)} %copy-done.47) | copy-start | bytes 196612
  791.4 11.4 %copy-start.68 = (f32[128,24]{0,1:T(8,128)S(1)}, f32[128,24]{0,1:T(8,128)}, u32[]{:S(2)}) copy-start(f32[128,24]{0,1:T(8,128)} %copy-done.66) | copy-start | bytes 36868
  791.4 11.4 %copy-start.74 = (f32[128,128]{0,1:T(8,128)S(1)}, f32[128,128]{0,1:T(8,128)}, u32[]{:S(2)}) copy-start(f32[128,128]{0,1:T(8,128)} %get-tuple-element.678) | copy-start | bytes 196612
  791.4 11.4 %copy-start.99 = (f32[128]{0:T(128)S(1)}, f32[128]{0:T(128)}, u32[]{:S(2)}) copy-start(f32[128]{0:T(128)} %param.25) | copy-start | bytes 1540
  791.4 11.4 %copy-start.101 = (f32[128]{0:T(128)S(1)}, f32[128]{0:T(128)}, u32[]{:S(2)}) copy-start(f32[128]{0:T(128)} %param.24) | copy-start | bytes 1540
  817.2 74.1 %copy-start.12 = (f32[128,4,768]{0,2,1:T(8,128)S(1)}, f32[128,4,768]{0,2,1:T(8,128)}, u32[]{:S(2)}) copy-start(f32[128,4,768]{0,2,1:T(8,128)} %copy-done.11) | copy-start | bytes 4718596
  817.2 74.1 %copy-start.76 = (f32[3072]{0:T(1024)S(1)}, f32[3072]{0:T(1024)}, u32[]{:S(2)}) copy-start(f32[3072]{0:T(1024)} %copy-done.75) | copy-start | bytes 36868
  817.2 74.1 %copy-start.78 = (f32[3072]{0:T(1024)S(1)}, f32[3072]{0:T(1024)}, u32[]{:S(2)}) copy-start(f32[3072]{0:T(1024)} %copy-done.77) | copy-start | bytes 36868
  (138 other events, 437.3 us)
Sparse Core Ops, SparseCore 0:
  12.3 57.3 all-gather.4
  72.2 77.0 all-gather.10
  152.5 53.5 all-gather.8
  208.4 50.2 all-gather.6
  562.4 88.5 all-reduce.1
  653.5 35.0 reduce-scatter.7
  691.1 35.1 reduce-scatter.5
  729.5 35.2 reduce-scatter.3
where the time goes:
time: 926 us; the launch traced here: 909 us
  waiting for transfers between devices  222 us (24%)
  local copies, waits for them, and re-layouts  194 us (21%)
  matrix products  156 us (17%)
  blocking collectives  126 us (14%)
  other arithmetic  77.8 us (8%)
  starting transfers between devices  69.5 us (8%)
  loops' own time  47.3 us (5%)
  between operations  16 us (2%)
    psum x1, blocking collectives, body(): lax.psum(jnp.stack([part_qv, part_kv, part_qt, part_kt]), ('slab', 'heads'))  71.1 us
    all_gather x1, waiting for transfers between devices, body(): lax.all_gather(v_text, ('slab', 'heads'), axis=0, tiled=True)  52.7 us
    concatenate x4, local copies, waits for them, and re-layouts, swap_halves(): return jnp.concatenate(pieces, axis=-1)  50.5 us
    dot_general x24, matrix products, contract_leading_axes(): lax.dot_general(first_op, second_op, (((0,), (0,)), ((), ())), preferred_...  47.8 us
    another operation x1, loops' own time, body(): lax.map(per_head, (split_heads(q_heads), split_heads(k_wide), split_heads...  47.3 us
    dot_general x24, matrix products, contract_last(): lax.dot_general(first_op, second_op, (((1,), (1,)), ((), ())), preferred_...  45.8 us
    all_gather x1, waiting for transfers between devices, body(): lax.all_gather(qt_norm, ('slab', 'heads'), axis=0, tiled=True)  45.1 us
    pmax x1, blocking collectives, body(): row_top = lax.pmax(local_top, 'slab')  40.2 us
  transfers between devices with their start and end apart: 24, of which 14 were waited for; matrix products, arithmetic and copies ran while one was open for 23% of the time, Pallas kernels for 0%

commit v1 on v0

v1 whole, which is shorter than its diff:
```python
import functools

import jax
import jax.numpy as jnp
from jax import lax
from jax.experimental import pallas as pl
from jax.experimental.pallas import tpu as pltpu
from jax.sharding import PartitionSpec as P

HEADS = 24
HD = 128
D = 3072
TEXT = 256
GRID_H = 16
GRID_W = 32

EPSILON = 1e-06
ROPE_BASE = 256.0
NEGATIVE = -1e30
FACTOR = HD ** (-0.5)
LOG2E = 1.4426950408889634
SHARP = FACTOR * LOG2E
MESH = pl.DeviceIdType.MESH
F32 = jnp.float32
BF16 = jnp.bfloat16


def section_list(head_dim):
    first_len = head_dim // 8
    other_len = 7 * head_dim // 16
    return ((0, first_len), (first_len, other_len), (first_len + other_len, other_len))


def rope_tables(token_index, head_dim):
    frame_at = token_index // (GRID_H * GRID_W)
    height = token_index // GRID_W % GRID_H
    across = token_index % GRID_W
    places = (frame_at, height, across)
    angles = []
    signs = []
    for number, (start_offset, length) in enumerate(section_list(head_dim)):
        half_len = length // 2
        offsets = (jnp.arange(length, dtype=jnp.int32) % half_len).astype(jnp.float32)
        frequency = jnp.power(jnp.float32(ROPE_BASE), -2.0 * offsets / length)
        angles.append(places[number].astype(jnp.float32)[:, None] * frequency[None, :])
        signs.append(jnp.where(jnp.arange(length) < half_len, -1.0, 1.0))
    angles = jnp.concatenate(angles, axis=1)
    signs = jnp.concatenate(signs)[None, :]
    return jnp.cos(angles), jnp.sin(angles) * signs


def head_order(windows, groups):
    local = HEADS // groups
    wide = windows[:, 0] == 3
    ids = jnp.arange(HEADS, dtype=jnp.int32)
    before = ids[None, :] < ids[:, None]
    rank_wide = jnp.sum(before & wide[None, :], axis=1, dtype=jnp.int32)
    rank_flat = jnp.sum(before & ~wide[None, :], axis=1, dtype=jnp.int32)
    slot = jnp.where(wide, rank_wide // groups, local // 2 + rank_flat // groups)
    group = jnp.where(wide, rank_wide % groups, rank_flat % groups)
    place = group * local + slot
    chosen = place[None, :] == ids[:, None]
    order = jnp.sum(jnp.where(chosen, ids[None, :], 0), axis=1, dtype=jnp.int32)
    reach = windows[:, 1:] // 2
    reach = jnp.sum(jnp.where(chosen[:, :, None], reach[None, :, :], 0), axis=1, dtype=jnp.int32)
    return order, place, reach.reshape(2 * HEADS)


def nt(a, b):
    return lax.dot_general(a, b, (((1,), (1,)), ((), ())), preferred_element_type=F32)


def nn(a, b):
    return lax.dot_general(a, b, (((1,), (0,)), ((), ())), preferred_element_type=F32)


def fold(values, op):
    return op(values.reshape(values.shape[0] // 8, 8, values.shape[1]), axis=0)


def partner(u):
    lane = lax.broadcasted_iota(jnp.int32, u.shape, 1)
    small = jnp.where(lane < 8, pltpu.roll(u, HD - 8, 1), pltpu.roll(u, 8, 1))
    first = ((lane >= 16) & (lane < 44)) | ((lane >= 72) & (lane < 100))
    large = jnp.where(first, pltpu.roll(u, HD - 28, 1), pltpu.roll(u, 28, 1))
    return jnp.where(lane < 16, small, large)


def inverse_rms(u):
    return lax.rsqrt(jnp.mean(u * u, axis=-1, keepdims=True) + EPSILON)


class Names:
    pass


def kernel(S, G, names, *refs):
    n = Names()
    for name, ref in zip(names, refs):
        setattr(n, name, ref)
    n.orecv = (n.orecv0, n.orecv1)
    L = HEADS // G
    LT = L // 2
    R = n.q.shape[0]
    N = R * G
    TD = n.qt.shape[0]
    TS = TD * G
    Z = S // 2
    s = lax.axis_index("slab")
    x = lax.axis_index("heads")
    zi = s // 2
    ci = lax.rem(s, 2)
    sib = s + 1 - 2 * ci

    def xdev(d):
        return lax.rem(x + d, G)

    def sdev(d):
        return lax.rem(s + d, S)

    def zdev(d):
        return lax.rem(zi + d, Z) * 2 + ci

    def copy(src, dst, ss, rs, dev):
        return pltpu.make_async_remote_copy(
            src_ref=src, dst_ref=dst, send_sem=ss, recv_sem=rs, device_id=dev, device_id_type=MESH
        )

    bar = pltpu.get_barrier_semaphore()
    for d in range(1, G):
        pl.semaphore_signal(bar, inc=1, device_id={"heads": xdev(d)}, device_id_type=MESH)
    for d in range(1, S):
        pl.semaphore_signal(bar, inc=1, device_id={"slab": sdev(d)}, device_id_type=MESH)

    def tx(d):
        return copy(
            n.tsend.at[d], n.tg.at[s, x], n.tx_s.at[d], n.tx_r.at[d], {"heads": xdev(d)}
        )

    def tx_in(d):
        src = lax.rem(x + G - d, G)
        return copy(n.tsend.at[d], n.tg.at[s, src], n.tx_s.at[d], n.tx_r.at[d], {"heads": src})

    def tgat(sem, slab, dev):
        return copy(n.tg.at[slab], n.tg.at[slab], n.tg_s.at[sem], n.tg_r.at[slab], {"slab": dev})

    def inp(i, d):
        return copy(
            n.send.at[i, d],
            n.recv.at[i, :, pl.ds(pl.multiple_of(x * R, R), R), :],
            n.in_s.at[i, d],
            n.in_r.at[i, d],
            {"heads": xdev(d)},
        )

    def inp_in(i, d):
        src = lax.rem(x + G - d, G)
        return copy(
            n.send.at[i, d],
            n.recv.at[i, :, pl.ds(pl.multiple_of(src * R, R), R), :],
            n.in_s.at[i, d],
            n.in_r.at[i, d],
            {"heads": src},
        )

    def halo(i, up):
        return copy(
            n.recv.at[i, pl.ds(1, 2)],
            n.halo.at[i, 0 if up else 1],
            n.ha_s.at[i, 1 if up else 0],
            n.ha_r.at[i, 0 if up else 1],
            {"slab": s + 1 if up else s - 1},
        )

    def halo_in(i, below):
        k = 0 if below else 1
        return copy(
            n.recv.at[i, pl.ds(1, 2)],
            n.halo.at[i, k],
            n.ha_s.at[i, k],
            n.ha_r.at[i, k],
            {"slab": s - 1 if below else s + 1},
        )

    def hgrad(i, up):
        k = 1 if up else 0
        return copy(
            n.hsend.at[i, k],
            n.hrecv.at[i, 1 - k],
            n.hg_s.at[i, k],
            n.hg_r.at[i, 1 - k],
            {"slab": s + 1 if up else s - 1},
        )

    def hgrad_in(i, below):
        k = 0 if below else 1
        return copy(
            n.hsend.at[i, k],
            n.hrecv.at[i, k],
            n.hg_s.at[i, k],
            n.hg_r.at[i, k],
            {"slab": s - 1 if below else s + 1},
        )

    def outp(a, i, d):
        j = xdev(d)
        return copy(
            n.osend.at[a, i, j],
            n.orecv[a].at[x * L + i],
            n.o_s.at[a, i, d],
            n.o_r.at[a, i, d],
            {"heads": j},
        )

    def outp_in(a, i, d):
        src = lax.rem(x + G - d, G)
        return copy(
            n.osend.at[a, i, src],
            n.orecv[a].at[src * L + i],
            n.o_s.at[a, i, d],
            n.o_r.at[a, i, d],
            {"heads": src},
        )

    def stat(d):
        return copy(n.stats.at[s], n.stats.at[s], n.st_s.at[d], n.st_r.at[d], {"slab": sdev(d)})

    def stat_in(d):
        src = lax.rem(s + S - d, S)
        return copy(n.stats.at[src], n.stats.at[src], n.st_s.at[d], n.st_r.at[d], {"slab": src})

    def pair(z):
        return copy(
            n.tpart.at[2 * z + 1 - ci], n.tsib.at[z], n.p_s.at[z], n.p_r.at[z], {"slab": sib}
        )

    def zred(d):
        return copy(
            n.tz.at[lax.rem(zi + d, Z)], n.tzr.at[d], n.z_s.at[d], n.z_r.at[d], {"slab": zdev(d)}
        )

    def tfin(d):
        return copy(
            n.tfs.at[xdev(d)],
            n.tfr.at[pl.ds(x * L, L)],
            n.tf_s.at[d],
            n.tf_r.at[d],
            {"heads": xdev(d)},
        )

    def tfin_in(d):
        src = lax.rem(x + G - d, G)
        return copy(
            n.tfs.at[src], n.tfr.at[pl.ds(src * L, L)], n.tf_s.at[d], n.tf_r.at[d], {"heads": src}
        )

    def gainx(d):
        return copy(n.gx.at[0], n.gx.at[d], n.gx_s.at[d], n.gx_r.at[d], {"heads": xdev(d)})

    def gains(d):
        return copy(n.gs.at[0], n.gs.at[d], n.gs_s.at[d], n.gs_r.at[d], {"slab": sdev(d)})

    def lanes(h):
        return pl.ds(pl.multiple_of(h * HD, HD), HD)

    def by_head(h, carry):
        for a, ref in enumerate((n.q, n.k, n.v, n.g)):
            n.raw[h, a] = ref[:, lanes(h)]
        for a, ref in enumerate((n.qt, n.kt, n.vt, n.gt)):
            n.rawt[h, a] = ref[:, lanes(h)].astype(F32)
        return carry

    lax.fori_loop(0, HEADS, by_head, 0)

    def text_pre(i, carry):
        for d in range(G):
            h = n.order[xdev(d) * L + i]
            uq = n.rawt[h, 0]
            uk = n.rawt[h, 1]
            a = jnp.concatenate(
                [uq * inverse_rms(uq) * n.gqt[...], uk * inverse_rms(uk) * n.gkt[...]], axis=0
            ).astype(BF16)
            b = jnp.concatenate([n.rawt[h, 2], n.rawt[h, 3]], axis=0).astype(BF16)
            if d == 0:
                n.tg[s, x, i, 0] = a
                n.tg[s, x, i, 1] = b
            else:
                n.tsend[d, i, 0] = a
                n.tsend[d, i, 1] = b
        return carry

    lax.fori_loop(0, L, text_pre, 0)
    pl.semaphore_wait(bar, G - 1 + S - 1)
    for d in range(1, G):
        tx(d).start()

    def normed(u, gain):
        u = u.astype(F32)
        y = u * inverse_rms(u) * gain
        return (y * n.cos[...] + partner(y) * n.sin[...]).astype(BF16)

    def video_pre(i, carry):
        for d in range(G):
            h = n.order[xdev(d) * L + i]
            rows = (
                normed(n.raw[h, 0], n.gqv[...]),
                normed(n.raw[h, 1], n.gkv[...]),
                n.raw[h, 2],
                n.raw[h, 3],
            )
            for a in range(4):
                if d == 0:
                    n.recv[i, a, pl.ds(pl.multiple_of(x * R, R), R), :] = rows[a]
                else:
                    n.send[i, d, a] = rows[a]
            if d:
                inp(i, d).start()
        return carry

    lax.fori_loop(0, 1, video_pre, 0)
    for d in range(1, G):
        tx_in(d).wait_recv()
    tgat(0, s, sib).start()
    for d in range(1, Z):
        tgat(d, s, zdev(d)).start()
    lax.fori_loop(1, L, video_pre, 0)

    row = lax.broadcasted_iota(jnp.int32, (N, HD), 0)
    lane = lax.broadcasted_iota(jnp.int32, (N, HD), 1)
    tile_row = row // (N // 2)
    tile_col = lax.rem(row, GRID_W) // 8
    n.qaug[:, HD:] = jnp.where(lane == tile_row * 4 + tile_col, 1.0, 0.0).astype(BF16)

    def forward_halo(i):
        for d in range(1, G):
            inp_in(i, d).wait_recv()

        @pl.when(s < S - 1)
        def _():
            halo(i, True).start()

        @pl.when(s > 0)
        def _():
            halo(i, False).start()

    forward_halo(0)
    for d in range(1, Z):
        src = zdev(d)
        tgat(Z + d, src, sib).wait_recv()
        tgat(Z + d, src, sib).start()
    forward_halo(1)
    tgat(0, sib, sib).wait_recv()
    for d in range(1, Z):
        other = lax.rem(zi + d, Z) * 2 + 1 - ci
        tgat(Z + d, other, sib).wait_recv()

    def text_take(i, carry):
        for p in range(2):
            both = n.tg[:, :, i, p].astype(F32).reshape(S * G, 2 * TD, HD)
            for k in range(2):
                n.text[i, 2 * p + k] = (
                    both[:, k * TD : (k + 1) * TD].reshape(TEXT, HD).astype(BF16)
                )
        return carry

    lax.fori_loop(0, L, text_take, 0)

    def key_rows(at, count, k_rows, v_rows, feature):
        n.kaug[at : at + count, :HD] = k_rows
        n.kaug[at : at + count, HD:] = feature
        n.vbuf[at : at + count, :] = v_rows

    def attend(i, chunks):
        reach_y = n.reach[2 * (x * L + i)]
        reach_x = n.reach[2 * (x * L + i) + 1]
        fits = (jnp.abs(tile_row - lane // 4) <= reach_y) & (
            jnp.abs(tile_col - lax.rem(lane, 4)) <= reach_x
        )
        feature = jnp.where(fits, 0.0, NEGATIVE).astype(BF16)
        n.qaug[:, :HD] = n.recv[i, 0]
        key_rows(0, N, n.recv[i, 1], n.recv[i, 2], feature)
        key_rows(N, TEXT, n.text[i, 1], n.text[i, 2], n.tbias[...])
        if chunks > 3:
            for k, below in ((0, True), (1, False)):
                at = N + TEXT + k * N
                here = (s > 0) if below else (s < S - 1)

                @pl.when(here)
                def _():
                    halo_in(i, below).wait_recv()
                    key_rows(at, N, n.halo[i, k, 0], n.halo[i, k, 1], feature)

                @pl.when(jnp.logical_not(here))
                def _():
                    zero = jnp.zeros((N, HD), BF16)
                    key_rows(at, N, zero, zero, jnp.full((N, HD), NEGATIVE, BF16))

        for c in range(chunks):
            at = slice(c * 256, (c + 1) * 256)
            n.kT[:, at] = n.kaug[at, :HD].T
            n.vT[:, at] = n.vbuf[at, :].T

        def block(b, carry):
            at_q = pl.ds(pl.multiple_of(b * 256, 256), 256)
            qa = n.qaug[at_q, :]
            qn = n.qaug[at_q, :HD]
            gb = n.recv[i, 3, at_q, :]
            top = jnp.full((8, 256), NEGATIVE, F32)
            for c in range(chunks):
                at = slice(c * 256, (c + 1) * 256)
                sc = nt(n.kaug[at, :], qa)
                n.sbuf[at, :] = sc
                top = jnp.maximum(top, fold(sc, jnp.max))
            top = jnp.max(top, axis=0, keepdims=True) * SHARP
            total = jnp.zeros((8, 256), F32)
            acc = jnp.zeros((HD, 256), F32)
            for c in range(chunks):
                at = slice(c * 256, (c + 1) * 256)
                e = jnp.exp2(n.sbuf[at, :] * SHARP - top)
                n.sbuf[at, :] = e
                total = total + fold(e, jnp.sum)
                w = e.astype(BF16)
                acc = acc + nn(n.vT[:, at], w)
                dv = nn(w, gb)
                if c * 256 < N:
                    n.dvm[i, at, :] += dv
                elif c * 256 < N + TEXT:
                    n.dvt[i, :, :] += dv
                else:
                    n.dvh[c * 256 - N - TEXT : (c + 1) * 256 - N - TEXT, :] += dv
            inv = 1.0 / jnp.sum(total, axis=0, keepdims=True)
            out = (acc * inv).astype(BF16)
            gT = gb.astype(F32).T
            dot = jnp.sum(fold(gT * out.astype(F32), jnp.sum), axis=0, keepdims=True)
            dq = jnp.zeros((HD, 256), F32)
            for c in range(chunks):
                at = slice(c * 256, (c + 1) * 256)
                dp = nt(n.vbuf[at, :], gb)
                ds = ((n.sbuf[at, :] * inv) * (dp - dot)).astype(BF16)
                dq = dq + nn(n.kT[:, at], ds)
                dk = nn(ds, qn)
                if c * 256 < N:
                    n.dkm[i, at, :] += dk
                elif c * 256 < N + TEXT:
                    n.dkt[i, :, :] += dk
                else:
                    n.dkh[c * 256 - N - TEXT : (c + 1) * 256 - N - TEXT, :] += dk
            out = out.astype(F32).T.astype(BF16)
            dq = (dq * FACTOR).T.astype(BF16)
            for j in range(256 // R):
                n.osend[0, i, b * (256 // R) + j, 0] = out[j * R : (j + 1) * R]
                n.osend[0, i, b * (256 // R) + j, 1] = dq[j * R : (j + 1) * R]
            return carry

        n.dvm[i] = jnp.zeros((N, HD), F32)
        n.dkm[i] = jnp.zeros((N, HD), F32)
        n.dvt[i] = jnp.zeros((TEXT, HD), F32)
        n.dkt[i] = jnp.zeros((TEXT, HD), F32)
        if chunks > 3:
            n.dvh[...] = jnp.zeros((2 * N, HD), F32)
            n.dkh[...] = jnp.zeros((2 * N, HD), F32)
        lax.fori_loop(0, N // 256, block, 0)

        for d in range(1, G):
            outp(0, i, d).start()
        n.orecv[0][x * L + i] = n.osend[0, i, x]
        if chunks > 3:
            for k in range(2):
                n.hsend[i, k, 0] = (n.dkh[k * N : (k + 1) * N, :] * FACTOR).astype(BF16)
                n.hsend[i, k, 1] = n.dvh[k * N : (k + 1) * N, :].astype(BF16)

            @pl.when(s < S - 1)
            def _():
                hgrad(i, True).start()

            @pl.when(s > 0)
            def _():
                hgrad(i, False).start()

    def attend_wide(i, carry):
        attend(i, (3 * N + TEXT) // 256)
        return carry

    def attend_flat(i, carry):
        attend(i, (N + TEXT) // 256)
        return carry

    share = pl.ds(pl.multiple_of(s * TS, TS), TS)
    share_bias = n.tbias[share, :].astype(F32)
    share_bias = jnp.concatenate([share_bias, share_bias], axis=1)

    def text_scores(i):
        sv = nt(n.recv[i, 1], n.text[i, 0])
        st = nt(n.text[i, 1, share, :], n.text[i, 0]) + share_bias
        pv = nt(n.recv[i, 2], n.text[i, 3])
        pt = nt(n.text[i, 2, share, :], n.text[i, 3])
        return sv, st, pv, pt

    def text_first(i, carry):
        sv, st, pv, pt = text_scores(i)
        top = jnp.maximum(fold(sv, jnp.max), fold(st, jnp.max))
        top = jnp.max(top, axis=0, keepdims=True)
        ev = jnp.exp2((sv - top) * SHARP)
        et = jnp.exp2((st - top) * SHARP)
        total = fold(ev, jnp.sum) + fold(et, jnp.sum)
        dot = fold(ev * pv, jnp.sum) + fold(et * pt, jnp.sum)
        n.stats[s, 0, pl.ds(i, 1), :] = top
        n.stats[s, 1, pl.ds(i, 1), :] = jnp.sum(total, axis=0, keepdims=True)
        n.stats[s, 2, pl.ds(i, 1), :] = jnp.sum(dot, axis=0, keepdims=True)
        return carry

    def text_second(i, carry):
        sv, st, pv, pt = text_scores(i)
        tops = [n.stats[k, 0, pl.ds(i, 1), :] for k in range(S)]
        top = functools.reduce(jnp.maximum, tops)
        total = jnp.zeros((1, TEXT), F32)
        dot = jnp.zeros((1, TEXT), F32)
        for k in range(S):
            scale = jnp.exp2((tops[k] - top) * SHARP)
            total = total + n.stats[k, 1, pl.ds(i, 1), :] * scale
            dot = dot + n.stats[k, 2, pl.ds(i, 1), :] * scale
        inv = 1.0 / total
        dot = dot * inv
        ev = jnp.exp2((sv - top) * SHARP)
        et = jnp.exp2((st - top) * SHARP)
        wv = ev.astype(BF16)
        wt = et.astype(BF16)
        dsv = (ev * inv * (pv - dot)).astype(BF16)
        dst = (et * inv * (pt - dot)).astype(BF16)
        qt_ = n.text[i, 0]
        gt_ = n.text[i, 3]
        n.dvm[i] += nn(wv, gt_)
        n.dkm[i] += nn(dsv, qt_)
        n.dvt[i, share, :] += nn(wt, gt_)
        n.dkt[i, share, :] += nn(dst, qt_)
        kt_ = n.recv[i, 1].T
        vt_ = n.recv[i, 2].T
        ktt = n.text[i, 1, share, :].astype(F32).T.astype(BF16)
        vtt = n.text[i, 2, share, :].astype(F32).T.astype(BF16)
        out = (nn(vt_, wv) + nn(vtt, wt)) * inv
        dq = (nn(kt_, dsv) + nn(ktt, dst)) * FACTOR
        n.tpart[:, 0, i] = out.T.astype(BF16).reshape(S, TS, HD)
        n.tpart[:, 1, i] = dq.T.astype(BF16).reshape(S, TS, HD)
        n.tpart[:, 2, i] = (n.dkt[i] * FACTOR).astype(BF16).reshape(S, TS, HD)
        n.tpart[:, 3, i] = n.dvt[i].astype(BF16).reshape(S, TS, HD)
        return carry

    lax.fori_loop(0, 1, attend_wide, 0)
    forward_halo(2)
    lax.fori_loop(1, LT, attend_wide, 0)
    for i in range(LT, L):
        for d in range(1, G):
            inp_in(i, d).wait_recv()
    n.stats[s] = jnp.zeros((3, 8, TEXT), F32)
    lax.fori_loop(0, L, text_first, 0)
    for d in range(1, S):
        stat(d).start()
    lax.fori_loop(LT, L, attend_flat, 0)
    for d in range(1, S):
        stat_in(d).wait_recv()
    lax.fori_loop(0, L, text_second, 0)
    for z in range(Z):
        pair(z).start()

    def finish(i, wide):
        def pack(dk, dv):
            for j in range(G):
                n.osend[1, i, j, 0] = dk[j * R : (j + 1) * R].astype(BF16)
                n.osend[1, i, j, 1] = dv[j * R : (j + 1) * R].astype(BF16)

        if wide:
            for k, below in ((0, True), (1, False)):

                @pl.when((s > 0) if below else (s < S - 1))
                def _():
                    hgrad_in(i, below).wait_recv()
                    n.dkm[i] += n.hrecv[i, k, 0].astype(F32) * (1.0 / FACTOR)
                    n.dvm[i] += n.hrecv[i, k, 1].astype(F32)

        pack(n.dkm[i] * FACTOR, n.dvm[i])
        for d in range(1, G):
            outp(1, i, d).start()
        n.orecv[1][x * L + i] = n.osend[1, i, x]

    def finish_flat(i, carry):
        finish(i, False)
        return carry

    def finish_wide(i, carry):
        finish(i, True)
        return carry

    lax.fori_loop(LT, L, finish_flat, 0)
    for z in range(Z):
        pair(z).wait_recv()
        n.tz[z] = (n.tpart[2 * z + ci].astype(F32) + n.tsib[z].astype(F32)).astype(BF16)
    for d in range(1, Z):
        zred(d).start()
    lax.fori_loop(0, LT, finish_wide, 0)

    for i in range(L):
        for d in range(1, G):
            outp_in(0, i, d).wait_recv()

    def norm_back(u, dy, gain):
        r = inverse_rms(u)
        unit = u * r
        y = dy * gain
        grad = r * (y - unit * jnp.mean(y * unit, axis=-1, keepdims=True))
        return grad.astype(BF16), dy * unit

    def unrotate(y):
        return y * n.cos[...] - partner(y) * n.sin[...]

    def post_q(h, carry):
        p = n.place[h]
        n.o_out[:, lanes(h)] = n.orecv[0][p, 0]
        dy = unrotate(n.orecv[0][p, 1].astype(F32))
        grad, part = norm_back(n.q[:, lanes(h)].astype(F32), dy, n.gqv[...])
        n.o_dq[:, lanes(h)] = grad
        return carry + fold(part, jnp.sum)

    zero = jnp.zeros((8, HD), F32)
    gain_qv = lax.fori_loop(0, HEADS, post_q, zero)

    for d in range(1, Z):
        zred(d).wait_recv()
    summed = n.tz[zi].astype(F32)
    for d in range(1, Z):
        summed = summed + n.tzr[d].astype(F32)
    for j in range(G):
        rows = slice(j * TD, (j + 1) * TD)
        for p in range(2):
            n.tfs[j, :, p] = jnp.concatenate(
                [summed[2 * p, :, rows], summed[2 * p + 1, :, rows]], axis=1
            ).astype(BF16)
    for d in range(1, G):
        tfin(d).start()
    n.tfr[pl.ds(x * L, L)] = n.tfs[x]

    for i in range(L):
        for d in range(1, G):
            outp_in(1, i, d).wait_recv()

    def post_k(h, carry):
        p = n.place[h]
        n.o_dv[:, lanes(h)] = n.orecv[1][p, 1]
        dy = unrotate(n.orecv[1][p, 0].astype(F32))
        grad, part = norm_back(n.k[:, lanes(h)].astype(F32), dy, n.gkv[...])
        n.o_dk[:, lanes(h)] = grad
        return carry + fold(part, jnp.sum)

    gain_kv = lax.fori_loop(0, HEADS, post_k, zero)

    for d in range(1, G):
        tfin_in(d).wait_recv()

    def post_t(h, carry):
        p = n.place[h]
        a = n.tfr[p, 0].astype(F32)
        b = n.tfr[p, 1].astype(F32)
        n.o_outt[:, lanes(h)] = a[:TD].astype(BF16)
        n.o_dvt[:, lanes(h)] = b[TD:].astype(BF16)
        grad, part_q = norm_back(n.qt[:, lanes(h)].astype(F32), a[TD:], n.gqt[...])
        n.o_dqt[:, lanes(h)] = grad
        grad, part_k = norm_back(n.kt[:, lanes(h)].astype(F32), b[:TD], n.gkt[...])
        n.o_dkt[:, lanes(h)] = grad
        return carry[0] + fold(part_q, jnp.sum), carry[1] + fold(part_k, jnp.sum)

    gain_qt, gain_kt = lax.fori_loop(0, HEADS, post_t, (zero, zero))

    parts = [
        jnp.sum(part, axis=0, keepdims=True) for part in (gain_qv, gain_kv, gain_qt, gain_kt)
    ]
    n.gx[0] = jnp.concatenate(parts + [jnp.zeros((4, HD), F32)], axis=0)
    for d in range(1, G):
        gainx(d).start()
    for d in range(1, G):
        gainx(d).wait_recv()
    n.gs[0] = functools.reduce(lambda a, b: a + b, [n.gx[d] for d in range(G)])
    for d in range(1, S):
        gains(d).start()
    for d in range(1, S):
        gains(d).wait_recv()
    gain = functools.reduce(lambda a, b: a + b, [n.gs[d] for d in range(S)])
    n.o_gqv[...] = gain[0:1]
    n.o_gkv[...] = gain[1:2]
    n.o_gqt[...] = gain[2:3]
    n.o_gkt[...] = gain[3:4]

    for d in range(1, G):
        tx(d).wait_send()
        tfin(d).wait_send()
        gainx(d).wait_send()
        for i in range(L):
            inp(i, d).wait_send()
            outp(0, i, d).wait_send()
            outp(1, i, d).wait_send()
    tgat(0, s, sib).wait_send()
    for d in range(1, Z):
        tgat(d, s, zdev(d)).wait_send()
        tgat(Z + d, zdev(d), sib).wait_send()
        zred(d).wait_send()
    for z in range(Z):
        pair(z).wait_send()
    for d in range(1, S):
        stat(d).wait_send()
        gains(d).wait_send()
    for i in range(LT):
        for up in (True, False):

            @pl.when((s < S - 1) if up else (s > 0))
            def _():
                halo(i, up).wait_send()
                hgrad(i, up).wait_send()


def body(S, G, *args):
    (q, k, v, g, qt, kt, vt, gt, gqv, gkv, gqt, gkt, windows, text_mask) = args
    slab = lax.axis_index("slab")
    group = lax.axis_index("heads")
    R = q.shape[0]
    TD = qt.shape[0]
    TS = TD * G
    N = R * G
    L = HEADS // G
    LT = L // 2
    Z = S // 2
    order, place, reach = head_order(windows, G)
    index = (slab * G + group) * R + jnp.arange(R, dtype=jnp.int32)
    cos, sin = rope_tables(index, HD)
    tbias = jnp.broadcast_to(
        jnp.where(text_mask == 1, 0.0, NEGATIVE).astype(BF16)[:, None], (TEXT, HD)
    )
    smem = pl.BlockSpec(memory_space=pltpu.SMEM)
    vmem = pl.BlockSpec(memory_space=pltpu.VMEM)
    operands = [
        ("order", order, smem),
        ("place", place, smem),
        ("reach", reach, smem),
        ("cos", cos, vmem),
        ("sin", sin, vmem),
        ("tbias", tbias, vmem),
        ("gqv", gqv.reshape(1, HD), vmem),
        ("gkv", gkv.reshape(1, HD), vmem),
        ("gqt", gqt.reshape(1, HD), vmem),
        ("gkt", gkt.reshape(1, HD), vmem),
        ("q", q, vmem),
        ("k", k, vmem),
        ("v", v, vmem),
        ("g", g, vmem),
        ("qt", qt, vmem),
        ("kt", kt, vmem),
        ("vt", vt, vmem),
        ("gt", gt, vmem),
    ]
    rows = jax.ShapeDtypeStruct((R, D), BF16)
    trows = jax.ShapeDtypeStruct((TD, D), BF16)
    gain = jax.ShapeDtypeStruct((1, HD), F32)
    outs = [
        ("o_out", rows),
        ("o_outt", trows),
        ("o_dq", rows),
        ("o_dk", rows),
        ("o_dv", rows),
        ("o_dqt", trows),
        ("o_dkt", trows),
        ("o_dvt", trows),
        ("o_gqv", gain),
        ("o_gkv", gain),
        ("o_gqt", gain),
        ("o_gkt", gain),
    ]
    V = pltpu.VMEM
    dma = pltpu.SemaphoreType.DMA
    K = 3 * N + TEXT
    scratch = [
        ("raw", V((HEADS, 4, R, HD), BF16)),
        ("rawt", V((HEADS, 4, TD, HD), F32)),
        ("tsend", V((G, L, 2, 2 * TD, HD), BF16)),
        ("tg", V((S, G, L, 2, 2 * TD, HD), BF16)),
        ("text", V((L, 4, TEXT, HD), BF16)),
        ("send", V((L, G, 4, R, HD), BF16)),
        ("recv", V((L, 4, N, HD), BF16)),
        ("halo", V((LT, 2, 2, N, HD), BF16)),
        ("hsend", V((LT, 2, 2, N, HD), BF16)),
        ("hrecv", V((LT, 2, 2, N, HD), BF16)),
        ("osend", V((2, L, G, 2, R, HD), BF16)),
        ("orecv0", V((HEADS, 2, R, HD), BF16)),
        ("orecv1", V((HEADS, 2, R, HD), BF16)),
        ("stats", V((S, 3, 8, TEXT), F32)),
        ("tpart", V((S, 4, L, TS, HD), BF16)),
        ("tsib", V((Z, 4, L, TS, HD), BF16)),
        ("tz", V((Z, 4, L, TS, HD), BF16)),
        ("tzr", V((Z, 4, L, TS, HD), BF16)),
        ("tfs", V((G, L, 2, 2 * TD, HD), BF16)),
        ("tfr", V((HEADS, 2, 2 * TD, HD), BF16)),
        ("gx", V((G, 8, HD), F32)),
        ("gs", V((S, 8, HD), F32)),
        ("qaug", V((N, 2 * HD), BF16)),
        ("kaug", V((K, 2 * HD), BF16)),
        ("vbuf", V((K, HD), BF16)),
        ("kT", V((HD, K), BF16)),
        ("vT", V((HD, K), BF16)),
        ("sbuf", V((K, 256), F32)),
        ("dvm", V((L, N, HD), F32)),
        ("dkm", V((L, N, HD), F32)),
        ("dvt", V((L, TEXT, HD), F32)),
        ("dkt", V((L, TEXT, HD), F32)),
        ("dvh", V((2 * N, HD), F32)),
        ("dkh", V((2 * N, HD), F32)),
        ("tx_s", dma((G,))),
        ("tx_r", dma((G,))),
        ("tg_s", dma((2 * Z,))),
        ("tg_r", dma((S,))),
        ("in_s", dma((L, G))),
        ("in_r", dma((L, G))),
        ("ha_s", dma((LT, 2))),
        ("ha_r", dma((LT, 2))),
        ("hg_s", dma((LT, 2))),
        ("hg_r", dma((LT, 2))),
        ("o_s", dma((2, L, G))),
        ("o_r", dma((2, L, G))),
        ("st_s", dma((S,))),
        ("st_r", dma((S,))),
        ("p_s", dma((Z,))),
        ("p_r", dma((Z,))),
        ("z_s", dma((Z,))),
        ("z_r", dma((Z,))),
        ("tf_s", dma((G,))),
        ("tf_r", dma((G,))),
        ("gx_s", dma((G,))),
        ("gx_r", dma((G,))),
        ("gs_s", dma((S,))),
        ("gs_r", dma((S,))),
    ]
    names = [o[0] for o in operands] + [o[0] for o in outs] + [o[0] for o in scratch]
    result = pl.pallas_call(
        functools.partial(kernel, S, G, names),
        out_shape=[o[1] for o in outs],
        in_specs=[o[2] for o in operands],
        out_specs=[vmem] * len(outs),
        scratch_shapes=[o[1] for o in scratch],
        compiler_params=pltpu.CompilerParams(
            collective_id=0, has_side_effects=True, vmem_limit_bytes=60 << 20
        ),
        cost_estimate=pl.CostEstimate(
            flops=7 * 10**9, bytes_accessed=7 * 10**6, transcendentals=5 * 10**6
        ),
    )(*[o[1] for o in operands])
    return tuple(result[:8]) + tuple(r.reshape(HD) for r in result[8:])


def solution(mesh):
    S = mesh.shape["slab"]
    G = mesh.shape["heads"]
    rows = P(("replica", "slab", "heads"), None)
    split = P("replica")
    return jax.shard_map(
        functools.partial(body, S, G),
        mesh=mesh,
        in_specs=(rows,) * 8 + (split,) * 4 + (P(), split),
        out_specs=(rows,) * 8 + (split,) * 4,
        check_vma=False,
    )
```

time: 926 us -> 148 us (0.16); the launches traced: 909 us -> 148 us
  waiting for transfers between devices: 222 us -> 0 us
  local copies, waits for them, and re-layouts: 194 us -> 13.3 us
  matrix products: 156 us -> 0 us
  Pallas kernels: 0 us -> 132 us
  blocking collectives: 126 us -> 0 us
  other arithmetic: 77.8 us -> 2.2 us
  starting transfers between devices: 69.5 us -> 0 us
  loops' own time: 47.3 us -> 0 us
  between operations: 16 us -> 0.79 us
    dot_general x84 -> x0, matrix products: 156 us -> none  [the longest x24 47.8 us: contract_leading_axes(): lax.dot_general(first_op, second_op, (((0,), (0,)), ((), ())), preferred_...]
    pallas_call x0 -> x1, Pallas kernels: none -> 132 us  [body(): pl.pallas_call(functools.partial(kernel, S, G, names), out_shape=[o[1] fo...]
    all_gather x4 -> x0, waiting for transfers between devices: 97.8 us -> none  [the longest x1 52.7 us: body(): lax.all_gather(v_text, ('slab', 'heads'), axis=0, tiled=True)]
    psum x2 -> x0, blocking collectives: 86.3 us -> none  [the longest x1 71.1 us: body(): lax.psum(jnp.stack([part_qv, part_kv, part_qt, part_kt]), ('slab', 'heads'))]
    reduce_scatter x3 -> x0, waiting for transfers between devices: 68 us -> none  [the longest x1 26.6 us: body(): lax.psum_scatter(grad_vt_all.astype(jnp.bfloat16), 'slab', scatter_dimens...]
    concatenate x4 -> x0, local copies, waits for them, and re-layouts: 50.5 us -> none  [swap_halves(): return jnp.concatenate(pieces, axis=-1)]
    all_to_all x12 -> x0, starting transfers between devices: 49.2 us -> none  [the longest x1 4.98 us: body(): lax.all_to_all(k_norm, 'heads', split_axis=1, concat_axis=0, tiled=True)]
    another operation x1 -> x0, loops' own time: 47.3 us -> none  [body(): lax.map(per_head, (split_heads(q_heads), split_heads(k_wide), split_heads...]
  transfers between devices with their start and end apart: 24 -> 0, of which waited for: 14 -> 0; matrix products, arithmetic and copies ran while one was open for 23% -> 0% of each run, Pallas kernels for 0% -> 0%
where the time goes in v1:
time: 148 us
  Pallas kernels  132 us (89%)
  local copies, waits for them, and re-layouts  13.3 us (9%)
  other arithmetic  2.2 us (1%)
    pallas_call x1, Pallas kernels, body(): pl.pallas_call(functools.partial(kernel, S, G, names), out_shape=[o[1] fo...  132 us
    unnamed x40, local copies, waits for them, and re-layouts  11.9 us

profile of v1, /device:TPU:1, one launch (start us, length us, event | category | flops | bytes accessed | tf_op | source)
XLA Modules:
  0.0 147.9 jit_solution(4642696186883934997)
XLA Ops:
  0.7 0.0 copy-start.9
  0.7 0.0 copy-start.8
  0.7 0.7 copy-done.9
  1.3 0.0 copy-done.8
  1.4 0.1 convert_reduce_fusion
  1.5 0.0 copy-start.7
  1.5 0.6 select_reduce_fusion.1.refs_0_
  2.2 0.1 pad_maximum_fusion.1
  2.3 0.0 copy-done.7
  2.3 0.1 select_reduce_fusion
  2.5 0.1 copy.28
  2.5 0.6 reshape.231.refs_2_
  3.2 0.1 broadcast_multiply_fusion.2
  3.2 0.7 broadcast_in_dim.88.refs_5_
  4.0 0.1 broadcast_multiply_fusion.1
  4.1 1.0 sine_multiply_fusion
  5.1 131.6 %shard_map.229 = (bf16[128,3072]{1,0:T(8,128)(2,1)}, bf16[8,3072]{1,0:T(8,128)(2,1)}, bf16[128,3072]{1,0:T(8,128)(2,1)}, bf16[128,3072]{1,0:T(8,128)(2,1)}, bf16...) custom-call(s32[24]{0:T(128)} %select_reduce_fusion.1.refs_0_, ...), custom_call_target="tpu_custom_call" | custom-call | flops 7000000000 | bytes 7000000 | tf_op jit(solution)/shard_map/pallas_call | solution.py:838
  136.7 0.0 copy-start.6
  136.7 0.0 copy-start.2
  136.7 2.1 %copy.41 = bf16[128,3072]{1,0:T(8,128)(2,1)} copy(bf16[128,3072]{1,0:T(8,128)(2,1)} %get-tuple-element.56) | data formatting | bytes 1572864
  138.8 0.0 copy-done.6
  138.8 0.6 copy.42
  139.5 0.0 copy-done.2
  139.5 0.0 copy-start.1
  139.5 0.9 copy.43
  140.3 0.5 copy-done.1
  140.9 0.0 copy-start
  140.9 0.9 copy.44
  141.8 0.5 copy-done
  142.3 0.0 copy-start.5
  142.3 0.9 copy.45
  143.2 0.0 copy-done.5
  143.2 0.0 copy-start.4
  143.2 0.6 copy.46
  143.8 0.2 copy-done.4
  144.0 0.0 copy-start.3
  144.0 0.6 copy.47
  144.6 0.2 copy-done.3
  144.8 0.0 copy-start.13
  144.8 0.6 copy.48
  145.4 0.0 copy-done.13
  145.4 0.5 copy.49
  146.0 0.2 copy-done.12
  146.1 0.5 copy.50
  146.6 0.2 copy-done.11
  146.8 0.5 copy.51
  147.3 0.1 copy-done.10
  147.4 0.5 copy.52
  (15 shorter events, 0.1 us)
Async XLA Ops:
  0.7 0.7 copy-start.9
  0.7 0.7 copy-start.8
  1.5 0.8 copy-start.7
  136.7 2.2 %copy-start.6 = (bf16[8,3072]{1,0:T(8,128)(2,1)S(1)}, bf16[8,3072]{1,0:T(8,128)(2,1)}, u32[]{:S(2)}) copy-start(bf16[8,3072]{1,0:T(8,128)(2,1)} %get-tuple-element.57) | copy-start | bytes 147460
  136.7 2.8 %copy-start.2 = (bf16[128,3072]{1,0:T(8,128)(2,1)S(1)}, bf16[128,3072]{1,0:T(8,128)(2,1)}, u32[]{:S(2)}) copy-start(bf16[128,3072]{1,0:T(8,128)(2,1)} %get-tuple-element.58) | copy-start | bytes 2359300
  139.5 1.4 copy-start.1
  140.9 1.4 copy-start
  142.3 0.9 copy-start.5
  143.2 0.8 copy-start.4
  144.0 0.8 copy-start.3
  144.8 0.6 copy-start.13
  145.4 0.7 copy-start.12
  146.1 0.7 copy-start.11
  146.8 0.6 copy-start.10

commit v2 on v1

--- a/solution.py
+++ b/solution.py
@@ -17,36 +17,13 @@
 EPSILON = 1e-06
 ROPE_BASE = 256.0
 NEGATIVE = -1e30
+MANY = 6
 FACTOR = HD ** (-0.5)
 LOG2E = 1.4426950408889634
 SHARP = FACTOR * LOG2E
 MESH = pl.DeviceIdType.MESH
 F32 = jnp.float32
 BF16 = jnp.bfloat16
-
-
-def section_list(head_dim):
-    first_len = head_dim // 8
-    other_len = 7 * head_dim // 16
-    return ((0, first_len), (first_len, other_len), (first_len + other_len, other_len))
-
-
-def rope_tables(token_index, head_dim):
-    frame_at = token_index // (GRID_H * GRID_W)
-    height = token_index // GRID_W % GRID_H
-    across = token_index % GRID_W
-    places = (frame_at, height, across)
-    angles = []
-    signs = []
-    for number, (start_offset, length) in enumerate(section_list(head_dim)):
-        half_len = length // 2
-        offsets = (jnp.arange(length, dtype=jnp.int32) % half_len).astype(jnp.float32)
-        frequency = jnp.power(jnp.float32(ROPE_BASE), -2.0 * offsets / length)
-        angles.append(places[number].astype(jnp.float32)[:, None] * frequency[None, :])
-        signs.append(jnp.where(jnp.arange(length) < half_len, -1.0, 1.0))
-    angles = jnp.concatenate(angles, axis=1)
-    signs = jnp.concatenate(signs)[None, :]
-    return jnp.cos(angles), jnp.sin(angles) * signs
 
 
 def head_order(windows, groups):
@@ -59,11 +36,10 @@
     slot = jnp.where(wide, rank_wide // groups, local // 2 + rank_flat // groups)
     group = jnp.where(wide, rank_wide % groups, rank_flat % groups)
     place = group * local + slot
+    code = ids + windows[:, 1] // 2 * 32 + windows[:, 2] // 2 * 64
     chosen = place[None, :] == ids[:, None]
-    order = jnp.sum(jnp.where(chosen, ids[None, :], 0), axis=1, dtype=jnp.int32)
-    reach = windows[:, 1:] // 2
-    reach = jnp.sum(jnp.where(chosen[:, :, None], reach[None, :, :], 0), axis=1, dtype=jnp.int32)
-    return order, place, reach.reshape(2 * HEADS)
+    code = jnp.sum(jnp.where(chosen, code[None, :], 0), axis=1, dtype=jnp.int32)
+    return code + place * 128
 
 
 def nt(a, b):
@@ -78,16 +54,33 @@
     return op(values.reshape(values.shape[0] // 8, 8, values.shape[1]), axis=0)
 
 
+def partner_lane(lane):
+    first = ((lane >= 16) & (lane < 44)) | ((lane >= 72) & (lane < 100))
+    small = jnp.where(lane < 8, lane + 8, lane - 8)
+    return jnp.where(lane < 16, small, jnp.where(first, lane + 28, lane - 28))
+
+
 def partner(u):
     lane = lax.broadcasted_iota(jnp.int32, u.shape, 1)
+    first = ((lane >= 16) & (lane < 44)) | ((lane >= 72) & (lane < 100))
     small = jnp.where(lane < 8, pltpu.roll(u, HD - 8, 1), pltpu.roll(u, 8, 1))
-    first = ((lane >= 16) & (lane < 44)) | ((lane >= 72) & (lane < 100))
     large = jnp.where(first, pltpu.roll(u, HD - 28, 1), pltpu.roll(u, 28, 1))
     return jnp.where(lane < 16, small, large)
 
 
-def inverse_rms(u):
-    return lax.rsqrt(jnp.mean(u * u, axis=-1, keepdims=True) + EPSILON)
+def rope_tables(frame, first_row, rows):
+    lane = lax.broadcasted_iota(jnp.int32, (rows, HD), 1)
+    row = lax.broadcasted_iota(jnp.int32, (rows, HD), 0)
+    short = lane < 16
+    middle = lane < 72
+    inside = jnp.where(short, lane, jnp.where(middle, lane - 16, lane - 72))
+    half = jnp.where(short, 8, 28)
+    offset = jnp.where(inside >= half, inside - half, inside)
+    place = jnp.where(short, frame, jnp.where(middle, first_row + row // GRID_W, lax.rem(row, GRID_W)))
+    rate = jnp.where(short, -1.0, -16.0 / 56.0)
+    angle = place.astype(F32) * jnp.exp2(offset.astype(F32) * rate)
+    sine = jnp.sin(angle)
+    return jnp.cos(angle), jnp.where(inside < half, -sine, sine)
 
 
 class Names:
@@ -132,17 +125,27 @@
     for d in range(1, S):
         pl.semaphore_signal(bar, inc=1, device_id={"slab": sdev(d)}, device_id_type=MESH)
 
-    def tx(d):
-        return copy(
-            n.tsend.at[d], n.tg.at[s, x], n.tx_s.at[d], n.tx_r.at[d], {"heads": xdev(d)}
-        )
-
-    def tx_in(d):
+    tg = (n.tg0, n.tg1)
+
+    def tx(p, d):
+        return copy(
+            n.tsend.at[p, d], tg[p].at[s, x], n.tx_s.at[p, d], n.tx_r.at[p, d], {"heads": xdev(d)}
+        )
+
+    def tx_in(p, d):
         src = lax.rem(x + G - d, G)
-        return copy(n.tsend.at[d], n.tg.at[s, src], n.tx_s.at[d], n.tx_r.at[d], {"heads": src})
-
-    def tgat(sem, slab, dev):
-        return copy(n.tg.at[slab], n.tg.at[slab], n.tg_s.at[sem], n.tg_r.at[slab], {"slab": dev})
+        return copy(
+            n.tsend.at[p, d], tg[p].at[s, src], n.tx_s.at[p, d], n.tx_r.at[p, d], {"heads": src}
+        )
+
+    def tgat(p, sem, slab, dev):
+        return copy(
+            tg[p].at[slab], tg[p].at[slab], n.tg_s.at[p, sem], n.tg_r.at[p, slab], {"slab": dev}
+        )
+
+    def trelay(p, half, src, dev):
+        rows = tg[p].at[src, pl.ds(half * (G // 2), G // 2)]
+        return copy(rows, rows, n.tg_s.at[p, 3 + half], n.tg_r.at[p, S + half], {"slab": dev})
 
     def inp(i, d):
         return copy(
@@ -222,22 +225,33 @@
             {"heads": src},
         )
 
+    def stat_pair():
+        return copy(n.stats.at[0], n.stats.at[1], n.st_s.at[0], n.st_r.at[0], {"slab": sib})
+
     def stat(d):
-        return copy(n.stats.at[s], n.stats.at[s], n.st_s.at[d], n.st_r.at[d], {"slab": sdev(d)})
+        at = n.chips.at[zi]
+        return copy(at, at, n.st_s.at[d], n.st_r.at[d], {"slab": zdev(d)})
 
     def stat_in(d):
-        src = lax.rem(s + S - d, S)
-        return copy(n.stats.at[src], n.stats.at[src], n.st_s.at[d], n.st_r.at[d], {"slab": src})
+        src = lax.rem(zi + Z - d, Z)
+        at = n.chips.at[src]
+        return copy(at, at, n.st_s.at[d], n.st_r.at[d], {"slab": src * 2 + ci})
 
     def pair(z):
         return copy(
             n.tpart.at[2 * z + 1 - ci], n.tsib.at[z], n.p_s.at[z], n.p_r.at[z], {"slab": sib}
         )
 
-    def zred(d):
-        return copy(
-            n.tz.at[lax.rem(zi + d, Z)], n.tzr.at[d], n.z_s.at[d], n.z_r.at[d], {"slab": zdev(d)}
-        )
+    def zred(k):
+        up = k % 2 == 0
+        to = lax.rem(zi + (1 if up else Z - 1), Z)
+        low = k in (0, 3, 4)
+        rows = pl.ds(0 if low else 2, 2)
+        if k < 2:
+            src, dst = n.tz.at[lax.rem(zi + 2, Z), rows], n.tzh.at[k]
+        else:
+            src, dst = n.tz.at[to, rows], n.tzr.at[k % 2, rows]
+        return copy(src, dst, n.z_s.at[k], n.z_r.at[k], {"slab": to * 2 + ci})
 
     def tfin(d):
         return copy(
@@ -260,70 +274,133 @@
     def gains(d):
         return copy(n.gs.at[0], n.gs.at[d], n.gs_s.at[d], n.gs_r.at[d], {"slab": sdev(d)})
 
+    def order(p):
+        return n.table[p] & 31
+
+    def place(h):
+        return n.table[h] >> 7
+
     def lanes(h):
         return pl.ds(pl.multiple_of(h * HD, HD), HD)
 
     def by_head(h, carry):
         for a, ref in enumerate((n.q, n.k, n.v, n.g)):
             n.raw[h, a] = ref[:, lanes(h)]
+        return carry
+
+    for h in range(HEADS):
         for a, ref in enumerate((n.qt, n.kt, n.vt, n.gt)):
-            n.rawt[h, a] = ref[:, lanes(h)].astype(F32)
-        return carry
-
-    lax.fori_loop(0, HEADS, by_head, 0)
+            n.rawt[a, h] = ref[:, h * HD : (h + 1) * HD].astype(F32)
+
+    k_lane = lax.broadcasted_iota(jnp.int32, (HD, HD), 0)
+    lane = lax.broadcasted_iota(jnp.int32, (HD, HD), 1)
+    n.swap[...] = jnp.where(k_lane == partner_lane(lane), 1.0, 0.0).astype(BF16)
+    n.mean[...] = jnp.full((2 * HD, HD), 1.0 / HD, BF16)
+    bias = jnp.where(n.tmask[...] == 1, 0.0, NEGATIVE)
+    n.tbias[...] = jnp.broadcast_to(bias, (HD, TEXT)).T.astype(BF16)
+
+    def lane_mean(values):
+        high = values.astype(BF16)
+        low = (values - high.astype(F32)).astype(BF16)
+        return nn(jnp.concatenate([high, low], axis=1), n.mean[...])
+
+    def inverse_rms(u):
+        return lax.rsqrt(lane_mean(u * u) + EPSILON)
+
+    for a, gain in ((0, n.gqt), (1, n.gkt)):
+        u = n.rawt[a].reshape(HEADS * TD, HD)
+        n.normt[a] = (u * inverse_rms(u) * gain[...]).reshape(HEADS, TD, HD)
 
     def text_pre(i, carry):
         for d in range(G):
-            h = n.order[xdev(d) * L + i]
-            uq = n.rawt[h, 0]
-            uk = n.rawt[h, 1]
-            a = jnp.concatenate(
-                [uq * inverse_rms(uq) * n.gqt[...], uk * inverse_rms(uk) * n.gkt[...]], axis=0
-            ).astype(BF16)
-            b = jnp.concatenate([n.rawt[h, 2], n.rawt[h, 3]], axis=0).astype(BF16)
-            if d == 0:
-                n.tg[s, x, i, 0] = a
-                n.tg[s, x, i, 1] = b
-            else:
-                n.tsend[d, i, 0] = a
-                n.tsend[d, i, 1] = b
+            h = order(xdev(d) * L + i)
+            rows = (
+                jnp.concatenate([n.normt[1, h], n.rawt[2, h]], axis=0).astype(BF16),
+                jnp.concatenate([n.normt[0, h], n.rawt[3, h]], axis=0).astype(BF16),
+            )
+            for p in range(2):
+                if d == 0:
+                    tg[p][s, x, i] = rows[p]
+                else:
+                    n.tsend[p, d, i] = rows[p]
         return carry
 
     lax.fori_loop(0, L, text_pre, 0)
     pl.semaphore_wait(bar, G - 1 + S - 1)
-    for d in range(1, G):
-        tx(d).start()
-
-    def normed(u, gain):
-        u = u.astype(F32)
-        y = u * inverse_rms(u) * gain
-        return (y * n.cos[...] + partner(y) * n.sin[...]).astype(BF16)
+    for p in range(2):
+        for d in range(1, G):
+            tx(p, d).start()
+    lax.fori_loop(0, HEADS, by_head, 0)
+    cos, sin = rope_tables(s, x * (R // GRID_W), R)
+    n.cos[...] = cos
+    n.sin[...] = sin
+    for k, gain in ((0, n.gqv), (1, n.gkv)):
+        n.gcos[k] = gain[...] * cos
+        n.gsin[k] = partner(jnp.broadcast_to(gain[...], (8, HD)))[0:1] * sin
+    def normed(u, k):
+        f = u.astype(F32)
+        y = f * n.gcos[k] + nn(u, n.swap[...]) * n.gsin[k]
+        return (y * inverse_rms(f)).astype(BF16)
 
     def video_pre(i, carry):
         for d in range(G):
-            h = n.order[xdev(d) * L + i]
-            rows = (
-                normed(n.raw[h, 0], n.gqv[...]),
-                normed(n.raw[h, 1], n.gkv[...]),
-                n.raw[h, 2],
-                n.raw[h, 3],
-            )
+            h = order(xdev(d) * L + i)
+            rows = (normed(n.raw[h, 0], 0), normed(n.raw[h, 1], 1), n.raw[h, 2], n.raw[h, 3])
             for a in range(4):
                 if d == 0:
                     n.recv[i, a, pl.ds(pl.multiple_of(x * R, R), R), :] = rows[a]
                 else:
                     n.send[i, d, a] = rows[a]
-            if d:
-                inp(i, d).start()
         return carry
 
+    def send_slot(i):
+        for d in range(1, G):
+            inp(i, d).start()
+
+    after, behind, across = zdev(1), zdev(Z - 1), zdev(2)
+
+    def text_out(p):
+        for d in range(1, G):
+            tx_in(p, d).wait_recv()
+        tgat(p, 1, s, after).start()
+        tgat(p, 2, s, behind).start()
+        tgat(p, 0, s, sib).start()
+
+    def text_relay(p):
+        tgat(p, 1, behind, behind).wait_recv()
+        trelay(p, 0, behind, after).start()
+        tgat(p, 5, behind, sib).start()
+        tgat(p, 2, after, after).wait_recv()
+        trelay(p, 1, after, behind).start()
+        tgat(p, 6, after, sib).start()
+
+    def text_forward(p):
+        trelay(p, 0, across, behind).wait_recv()
+        trelay(p, 1, across, after).wait_recv()
+        tgat(p, 7, across, sib).start()
+
+    def text_in(p):
+        tgat(p, 0, sib, sib).wait_recv()
+        for d in range(1, Z):
+            other = lax.rem(zi + d, Z) * 2 + 1 - ci
+            tgat(p, 0, other, sib).wait_recv()
+
+        def text_take(i, carry):
+            both = tg[p][:, :, i].astype(F32).reshape(S * G, 2 * TD, HD)
+            for k in range(2):
+                n.text[i, 2 * p + k] = (
+                    both[:, k * TD : (k + 1) * TD].reshape(TEXT, HD).astype(BF16)
+                )
+            return carry
+
+        lax.fori_loop(0, L, text_take, 0)
+
     lax.fori_loop(0, 1, video_pre, 0)
-    for d in range(1, G):
-        tx_in(d).wait_recv()
-    tgat(0, s, sib).start()
-    for d in range(1, Z):
-        tgat(d, s, zdev(d)).start()
-    lax.fori_loop(1, L, video_pre, 0)
+    send_slot(0)
+    lax.fori_loop(1, 2, video_pre, 0)
+    text_out(0)
+    send_slot(1)
+    lax.fori_loop(2, L, video_pre, 0)
 
     row = lax.broadcasted_iota(jnp.int32, (N, HD), 0)
     lane = lax.broadcasted_iota(jnp.int32, (N, HD), 1)
@@ -334,6 +411,7 @@
     def forward_halo(i):
         for d in range(1, G):
             inp_in(i, d).wait_recv()
+        send_slot(i + 2)
 
         @pl.when(s < S - 1)
         def _():
@@ -342,28 +420,6 @@
         @pl.when(s > 0)
         def _():
             halo(i, False).start()
-
-    forward_halo(0)
-    for d in range(1, Z):
-        src = zdev(d)
-        tgat(Z + d, src, sib).wait_recv()
-        tgat(Z + d, src, sib).start()
-    forward_halo(1)
-    tgat(0, sib, sib).wait_recv()
-    for d in range(1, Z):
-        other = lax.rem(zi + d, Z) * 2 + 1 - ci
-        tgat(Z + d, other, sib).wait_recv()
-
-    def text_take(i, carry):
-        for p in range(2):
-            both = n.tg[:, :, i, p].astype(F32).reshape(S * G, 2 * TD, HD)
-            for k in range(2):
-                n.text[i, 2 * p + k] = (
-                    both[:, k * TD : (k + 1) * TD].reshape(TEXT, HD).astype(BF16)
-                )
-        return carry
-
-    lax.fori_loop(0, L, text_take, 0)
 
     def key_rows(at, count, k_rows, v_rows, feature):
         n.kaug[at : at + count, :HD] = k_rows
@@ -371,15 +427,15 @@
         n.vbuf[at : at + count, :] = v_rows
 
     def attend(i, chunks):
-        reach_y = n.reach[2 * (x * L + i)]
-        reach_x = n.reach[2 * (x * L + i) + 1]
+        reach_y = (n.table[x * L + i] >> 5) & 1
+        reach_x = (n.table[x * L + i] >> 6) & 1
         fits = (jnp.abs(tile_row - lane // 4) <= reach_y) & (
             jnp.abs(tile_col - lax.rem(lane, 4)) <= reach_x
         )
         feature = jnp.where(fits, 0.0, NEGATIVE).astype(BF16)
         n.qaug[:, :HD] = n.recv[i, 0]
         key_rows(0, N, n.recv[i, 1], n.recv[i, 2], feature)
-        key_rows(N, TEXT, n.text[i, 1], n.text[i, 2], n.tbias[...])
+        key_rows(N, TEXT, n.text[i, 0], n.text[i, 1], n.tbias[...])
         if chunks > 3:
             for k, below in ((0, True), (1, False)):
                 at = N + TEXT + k * N
@@ -477,23 +533,15 @@
             def _():
                 hgrad(i, False).start()
 
-    def attend_wide(i, carry):
-        attend(i, (3 * N + TEXT) // 256)
-        return carry
-
-    def attend_flat(i, carry):
-        attend(i, (N + TEXT) // 256)
-        return carry
-
     share = pl.ds(pl.multiple_of(s * TS, TS), TS)
     share_bias = n.tbias[share, :].astype(F32)
     share_bias = jnp.concatenate([share_bias, share_bias], axis=1)
 
     def text_scores(i):
-        sv = nt(n.recv[i, 1], n.text[i, 0])
-        st = nt(n.text[i, 1, share, :], n.text[i, 0]) + share_bias
+        sv = nt(n.recv[i, 1], n.text[i, 2])
+        st = nt(n.text[i, 0, share, :], n.text[i, 2]) + share_bias
         pv = nt(n.recv[i, 2], n.text[i, 3])
-        pt = nt(n.text[i, 2, share, :], n.text[i, 3])
+        pt = nt(n.text[i, 1, share, :], n.text[i, 3])
         return sv, st, pv, pt
 
     def text_first(i, carry):
@@ -504,21 +552,21 @@
         et = jnp.exp2((st - top) * SHARP)
         total = fold(ev, jnp.sum) + fold(et, jnp.sum)
         dot = fold(ev * pv, jnp.sum) + fold(et * pt, jnp.sum)
-        n.stats[s, 0, pl.ds(i, 1), :] = top
-        n.stats[s, 1, pl.ds(i, 1), :] = jnp.sum(total, axis=0, keepdims=True)
-        n.stats[s, 2, pl.ds(i, 1), :] = jnp.sum(dot, axis=0, keepdims=True)
+        n.stats[0, 0, pl.ds(i, 1), :] = top
+        n.stats[0, 1, pl.ds(i, 1), :] = jnp.sum(total, axis=0, keepdims=True)
+        n.stats[0, 2, pl.ds(i, 1), :] = jnp.sum(dot, axis=0, keepdims=True)
         return carry
 
     def text_second(i, carry):
         sv, st, pv, pt = text_scores(i)
-        tops = [n.stats[k, 0, pl.ds(i, 1), :] for k in range(S)]
+        tops = [n.chips[k, 0, pl.ds(i, 1), :] for k in range(Z)]
         top = functools.reduce(jnp.maximum, tops)
         total = jnp.zeros((1, TEXT), F32)
         dot = jnp.zeros((1, TEXT), F32)
-        for k in range(S):
+        for k in range(Z):
             scale = jnp.exp2((tops[k] - top) * SHARP)
-            total = total + n.stats[k, 1, pl.ds(i, 1), :] * scale
-            dot = dot + n.stats[k, 2, pl.ds(i, 1), :] * scale
+            total = total + n.chips[k, 1, pl.ds(i, 1), :] * scale
+            dot = dot + n.chips[k, 2, pl.ds(i, 1), :] * scale
         inv = 1.0 / total
         dot = dot * inv
         ev = jnp.exp2((sv - top) * SHARP)
@@ -527,7 +575,7 @@
         wt = et.astype(BF16)
         dsv = (ev * inv * (pv - dot)).astype(BF16)
         dst = (et * inv * (pt - dot)).astype(BF16)
-        qt_ = n.text[i, 0]
+        qt_ = n.text[i, 2]
         gt_ = n.text[i, 3]
         n.dvm[i] += nn(wv, gt_)
         n.dkm[i] += nn(dsv, qt_)
@@ -535,8 +583,8 @@
         n.dkt[i, share, :] += nn(dst, qt_)
         kt_ = n.recv[i, 1].T
         vt_ = n.recv[i, 2].T
-        ktt = n.text[i, 1, share, :].astype(F32).T.astype(BF16)
-        vtt = n.text[i, 2, share, :].astype(F32).T.astype(BF16)
+        ktt = n.text[i, 0, share, :].astype(F32).T.astype(BF16)
+        vtt = n.text[i, 1, share, :].astype(F32).T.astype(BF16)
         out = (nn(vt_, wv) + nn(vtt, wt)) * inv
         dq = (nn(kt_, dsv) + nn(ktt, dst)) * FACTOR
         n.tpart[:, 0, i] = out.T.astype(BF16).reshape(S, TS, HD)
@@ -545,18 +593,58 @@
         n.tpart[:, 3, i] = n.dvt[i].astype(BF16).reshape(S, TS, HD)
         return carry
 
-    lax.fori_loop(0, 1, attend_wide, 0)
+    forward_halo(0)
+    text_relay(0)
+    text_out(1)
+    forward_halo(1)
+    text_forward(0)
     forward_halo(2)
-    lax.fori_loop(1, LT, attend_wide, 0)
-    for i in range(LT, L):
+    text_relay(1)
+    text_in(0)
+
+    def slot_in(i):
         for d in range(1, G):
             inp_in(i, d).wait_recv()
-    n.stats[s] = jnp.zeros((3, 8, TEXT), F32)
-    lax.fori_loop(0, L, text_first, 0)
-    for d in range(1, S):
-        stat(d).start()
-    lax.fori_loop(LT, L, attend_flat, 0)
-    for d in range(1, S):
+
+    def attend_pair(i, carry):
+        @pl.when(i == 1)
+        def _():
+            text_forward(1)
+
+        @pl.when(i == LT - 1)
+        def _():
+            text_in(1)
+            slot_in(L - 1)
+            n.stats[0] = jnp.zeros((3, 8, TEXT), F32)
+            lax.fori_loop(0, L, text_first, 0)
+            stat_pair().start()
+
+        attend(i, (3 * N + TEXT) // 256)
+
+        @pl.when(i == LT - 1)
+        def _():
+            stat_pair().wait_recv()
+            top = jnp.maximum(n.stats[0, 0], n.stats[1, 0])
+            scales = [jnp.exp2((n.stats[k, 0] - top) * SHARP) for k in range(2)]
+            n.chips[zi, 0] = top
+            for a in (1, 2):
+                n.chips[zi, a] = n.stats[0, a] * scales[0] + n.stats[1, a] * scales[1]
+            for d in range(1, Z):
+                stat(d).start()
+
+        @pl.when(i < LT - 1)
+        def _():
+            slot_in(LT + i)
+
+        @pl.when(i == 0)
+        def _():
+            send_slot(L - 1)
+
+        attend(LT + i, (N + TEXT) // 256)
+        return carry
+
+    lax.fori_loop(0, LT, attend_pair, 0)
+    for d in range(1, Z):
         stat_in(d).wait_recv()
     lax.fori_loop(0, L, text_second, 0)
     for z in range(Z):
@@ -590,44 +678,63 @@
         finish(i, True)
         return carry
 
+    def relay_sums():
+        for k in range(2):
+            to = lax.rem(zi + (1 if k == 0 else Z - 1), Z)
+            rows = slice(2 * k, 2 * k + 2)
+            zred(k).wait_recv()
+            n.tz[to, rows] = (n.tz[to, rows].astype(F32) + n.tzh[k].astype(F32)).astype(BF16)
+            zred(4 + k).start()
+
     lax.fori_loop(LT, L, finish_flat, 0)
     for z in range(Z):
         pair(z).wait_recv()
         n.tz[z] = (n.tpart[2 * z + ci].astype(F32) + n.tsib[z].astype(F32)).astype(BF16)
-    for d in range(1, Z):
-        zred(d).start()
-    lax.fori_loop(0, LT, finish_wide, 0)
+    for k in range(4):
+        zred(k).start()
+    lax.fori_loop(0, LT - 1, finish_wide, 0)
+    relay_sums()
+    lax.fori_loop(LT - 1, LT, finish_wide, 0)
 
     for i in range(L):
         for d in range(1, G):
             outp_in(0, i, d).wait_recv()
 
     def norm_back(u, dy, gain):
-        r = inverse_rms(u)
-        unit = u * r
-        y = dy * gain
-        grad = r * (y - unit * jnp.mean(y * unit, axis=-1, keepdims=True))
-        return grad.astype(BF16), dy * unit
-
-    def unrotate(y):
-        return y * n.cos[...] - partner(y) * n.sin[...]
-
-    def post_q(h, carry):
-        p = n.place[h]
-        n.o_out[:, lanes(h)] = n.orecv[0][p, 0]
-        dy = unrotate(n.orecv[0][p, 1].astype(F32))
-        grad, part = norm_back(n.q[:, lanes(h)].astype(F32), dy, n.gqv[...])
-        n.o_dq[:, lanes(h)] = grad
+        f = u.astype(F32)
+        r = inverse_rms(f)
+        unit = f * r
+        part = dy * unit
+        return r * (dy * gain - unit * lane_mean(part * gain)), part
+
+    cos_many = jnp.concatenate([n.cos[...]] * MANY, axis=0)
+    sin_many = jnp.concatenate([n.sin[...]] * MANY, axis=0)
+
+    def post(step, carry, received, back, plain, source, gain, out_plain, out_grad):
+        heads = [MANY * step + k for k in range(MANY)]
+        places = [place(h) for h in heads]
+        for h, p in zip(heads, places):
+            out_plain[:, lanes(h)] = received[p, plain]
+        y = jnp.concatenate([received[p, back] for p in places], axis=0)
+        u = jnp.concatenate([source[:, lanes(h)] for h in heads], axis=0)
+        dy = y.astype(F32) * cos_many - nn(y, n.swap[...]) * sin_many
+        grad, part = norm_back(u, dy, gain[...])
+        for k, h in enumerate(heads):
+            out_grad[:, lanes(h)] = grad[k * R : (k + 1) * R].astype(BF16)
         return carry + fold(part, jnp.sum)
 
+    def post_q(step, carry):
+        return post(step, carry, n.orecv[0], 1, 0, n.q, n.gqv, n.o_out, n.o_dq)
+
+    def post_k(step, carry):
+        return post(step, carry, n.orecv[1], 0, 1, n.k, n.gkv, n.o_dv, n.o_dk)
+
     zero = jnp.zeros((8, HD), F32)
-    gain_qv = lax.fori_loop(0, HEADS, post_q, zero)
-
-    for d in range(1, Z):
-        zred(d).wait_recv()
-    summed = n.tz[zi].astype(F32)
-    for d in range(1, Z):
-        summed = summed + n.tzr[d].astype(F32)
+    gain_qv = lax.fori_loop(0, HEADS // MANY, post_q, zero)
+
+    for k in range(2, 6):
+        zred(k).wait_recv()
+    summed = n.tz[zi].astype(F32) + n.tzr[0].astype(F32) + n.tzr[1].astype(F32)
     for j in range(G):
         rows = slice(j * TD, (j + 1) * TD)
         for p in range(2):
@@ -642,39 +749,44 @@
         for d in range(1, G):
             outp_in(1, i, d).wait_recv()
 
-    def post_k(h, carry):
-        p = n.place[h]
-        n.o_dv[:, lanes(h)] = n.orecv[1][p, 1]
-        dy = unrotate(n.orecv[1][p, 0].astype(F32))
-        grad, part = norm_back(n.k[:, lanes(h)].astype(F32), dy, n.gkv[...])
-        n.o_dk[:, lanes(h)] = grad
-        return carry + fold(part, jnp.sum)
-
-    gain_kv = lax.fori_loop(0, HEADS, post_k, zero)
-
+    gain_kv = lax.fori_loop(0, HEADS // MANY, post_k, zero)
+
+    def text_order(p, carry):
+        h = order(p)
+        n.rawp[0, p] = n.rawt[0, h]
+        n.rawp[1, p] = n.rawt[1, h]
+        return carry
+
+    lax.fori_loop(0, HEADS, text_order, 0)
     for d in range(1, G):
         tfin_in(d).wait_recv()
 
+    first = n.tfr[:, 0].astype(F32)
+    second = n.tfr[:, 1].astype(F32)
+    n.tres[0] = first[:, :TD]
+    n.tres[3] = second[:, TD:]
+    gain_t = []
+    for k, dy, gain in ((0, first[:, TD:], n.gqt), (1, second[:, :TD], n.gkt)):
+        u = n.rawp[k].reshape(HEADS * TD, HD)
+        grad, part = norm_back(u, dy.reshape(HEADS * TD, HD), gain[...])
+        n.tres[1 + k] = grad.reshape(HEADS, TD, HD)
+        gain_t.append(fold(part, jnp.sum))
+
     def post_t(h, carry):
-        p = n.place[h]
-        a = n.tfr[p, 0].astype(F32)
-        b = n.tfr[p, 1].astype(F32)
-        n.o_outt[:, lanes(h)] = a[:TD].astype(BF16)
-        n.o_dvt[:, lanes(h)] = b[TD:].astype(BF16)
-        grad, part_q = norm_back(n.qt[:, lanes(h)].astype(F32), a[TD:], n.gqt[...])
-        n.o_dqt[:, lanes(h)] = grad
-        grad, part_k = norm_back(n.kt[:, lanes(h)].astype(F32), b[:TD], n.gkt[...])
-        n.o_dkt[:, lanes(h)] = grad
-        return carry[0] + fold(part_q, jnp.sum), carry[1] + fold(part_k, jnp.sum)
-
-    gain_qt, gain_kt = lax.fori_loop(0, HEADS, post_t, (zero, zero))
+        p = place(h)
+        n.o_outt[:, lanes(h)] = n.tres[0, p].astype(BF16)
+        n.o_dqt[:, lanes(h)] = n.tres[1, p].astype(BF16)
+        n.o_dkt[:, lanes(h)] = n.tres[2, p].astype(BF16)
+        n.o_dvt[:, lanes(h)] = n.tres[3, p].astype(BF16)
+        return carry
 
     parts = [
-        jnp.sum(part, axis=0, keepdims=True) for part in (gain_qv, gain_kv, gain_qt, gain_kt)
+        jnp.sum(part, axis=0, keepdims=True) for part in (gain_qv, gain_kv, *gain_t)
     ]
     n.gx[0] = jnp.concatenate(parts + [jnp.zeros((4, HD), F32)], axis=0)
     for d in range(1, G):
         gainx(d).start()
+    lax.fori_loop(0, HEADS, post_t, 0)
     for d in range(1, G):
         gainx(d).wait_recv()
     n.gs[0] = functools.reduce(lambda a, b: a + b, [n.gx[d] for d in range(G)])
@@ -689,22 +801,27 @@
     n.o_gkt[...] = gain[3:4]
 
     for d in range(1, G):
-        tx(d).wait_send()
+        tx(0, d).wait_send()
+        tx(1, d).wait_send()
         tfin(d).wait_send()
         gainx(d).wait_send()
         for i in range(L):
             inp(i, d).wait_send()
             outp(0, i, d).wait_send()
             outp(1, i, d).wait_send()
-    tgat(0, s, sib).wait_send()
-    for d in range(1, Z):
-        tgat(d, s, zdev(d)).wait_send()
-        tgat(Z + d, zdev(d), sib).wait_send()
-        zred(d).wait_send()
+    for p in range(2):
+        for sem in (0, 1, 2, 5, 6, 7):
+            tgat(p, sem, s, sib).wait_send()
+        for half in range(2):
+            trelay(p, half, s, sib).wait_send()
+    for k in range(6):
+        zred(k).wait_send()
     for z in range(Z):
         pair(z).wait_send()
+    stat_pair().wait_send()
+    for d in range(1, Z):
+        stat(d).wait_send()
     for d in range(1, S):
-        stat(d).wait_send()
         gains(d).wait_send()
     for i in range(LT):
         for up in (True, False):
@@ -715,10 +832,27 @@
                 hgrad(i, up).wait_send()
 
 
+def hand_on(count, *refs):
+    held = refs[2 * count : 3 * count]
+    sem = refs[-1]
+    copies = [
+        (
+            pltpu.make_async_copy(refs[k], held[k], sem.at[0, k]),
+            pltpu.make_async_copy(held[k], refs[count + k], sem.at[1, k]),
+        )
+        for k in range(count)
+    ]
+    for one, _ in copies:
+        one.start()
+    for one, two in copies:
+        one.wait()
+        two.start()
+    for _, two in copies:
+        two.wait()
+
+
 def body(S, G, *args):
     (q, k, v, g, qt, kt, vt, gt, gqv, gkv, gqt, gkt, windows, text_mask) = args
-    slab = lax.axis_index("slab")
-    group = lax.axis_index("heads")
     R = q.shape[0]
     TD = qt.shape[0]
     TS = TD * G
@@ -726,21 +860,11 @@
     L = HEADS // G
     LT = L // 2
     Z = S // 2
-    order, place, reach = head_order(windows, G)
-    index = (slab * G + group) * R + jnp.arange(R, dtype=jnp.int32)
-    cos, sin = rope_tables(index, HD)
-    tbias = jnp.broadcast_to(
-        jnp.where(text_mask == 1, 0.0, NEGATIVE).astype(BF16)[:, None], (TEXT, HD)
-    )
     smem = pl.BlockSpec(memory_space=pltpu.SMEM)
     vmem = pl.BlockSpec(memory_space=pltpu.VMEM)
     operands = [
-        ("order", order, smem),
-        ("place", place, smem),
-        ("reach", reach, smem),
-        ("cos", cos, vmem),
-        ("sin", sin, vmem),
-        ("tbias", tbias, vmem),
+        ("table", head_order(windows, G), smem),
+        ("tmask", text_mask.reshape(1, TEXT), vmem),
         ("gqv", gqv.reshape(1, HD), vmem),
         ("gkv", gkv.reshape(1, HD), vmem),
         ("gqt", gqt.reshape(1, HD), vmem),
@@ -776,9 +900,20 @@
     K = 3 * N + TEXT
     scratch = [
         ("raw", V((HEADS, 4, R, HD), BF16)),
-        ("rawt", V((HEADS, 4, TD, HD), F32)),
-        ("tsend", V((G, L, 2, 2 * TD, HD), BF16)),
-        ("tg", V((S, G, L, 2, 2 * TD, HD), BF16)),
+        ("rawt", V((4, HEADS, TD, HD), F32)),
+        ("normt", V((2, HEADS, TD, HD), F32)),
+        ("rawp", V((2, HEADS, TD, HD), F32)),
+        ("tres", V((4, HEADS, TD, HD), F32)),
+        ("swap", V((HD, HD), BF16)),
+        ("mean", V((2 * HD, HD), BF16)),
+        ("cos", V((R, HD), F32)),
+        ("sin", V((R, HD), F32)),
+        ("gcos", V((2, R, HD), F32)),
+        ("gsin", V((2, R, HD), F32)),
+        ("tbias", V((TEXT, HD), BF16)),
+        ("tsend", V((2, G, L, 2 * TD, HD), BF16)),
+        ("tg0", V((S, G, L, 2 * TD, HD), BF16)),
+        ("tg1", V((S, G, L, 2 * TD, HD), BF16)),
         ("text", V((L, 4, TEXT, HD), BF16)),
         ("send", V((L, G, 4, R, HD), BF16)),
         ("recv", V((L, 4, N, HD), BF16)),
@@ -788,11 +923,13 @@
         ("osend", V((2, L, G, 2, R, HD), BF16)),
         ("orecv0", V((HEADS, 2, R, HD), BF16)),
         ("orecv1", V((HEADS, 2, R, HD), BF16)),
-        ("stats", V((S, 3, 8, TEXT), F32)),
+        ("stats", V((2, 3, 8, TEXT), F32)),
+        ("chips", V((Z, 3, 8, TEXT), F32)),
         ("tpart", V((S, 4, L, TS, HD), BF16)),
         ("tsib", V((Z, 4, L, TS, HD), BF16)),
         ("tz", V((Z, 4, L, TS, HD), BF16)),
-        ("tzr", V((Z, 4, L, TS, HD), BF16)),
+        ("tzr", V((2, 4, L, TS, HD), BF16)),
+        ("tzh", V((2, 2, L, TS, HD), BF16)),
         ("tfs", V((G, L, 2, 2 * TD, HD), BF16)),
         ("tfr", V((HEADS, 2, 2 * TD, HD), BF16)),
         ("gx", V((G, 8, HD), F32)),
@@ -809,10 +946,10 @@
         ("dkt", V((L, TEXT, HD), F32)),
         ("dvh", V((2 * N, HD), F32)),
         ("dkh", V((2 * N, HD), F32)),
-        ("tx_s", dma((G,))),
-        ("tx_r", dma((G,))),
-        ("tg_s", dma((2 * Z,))),
-        ("tg_r", dma((S,))),
+        ("tx_s", dma((2, G))),
+        ("tx_r", dma((2, G))),
+        ("tg_s", dma((2, 8))),
+        ("tg_r", dma((2, S + 2))),
         ("in_s", dma((L, G))),
         ("in_r", dma((L, G))),
         ("ha_s", dma((LT, 2))),
@@ -821,12 +958,12 @@
         ("hg_r", dma((LT, 2))),
         ("o_s", dma((2, L, G))),
         ("o_r", dma((2, L, G))),
-        ("st_s", dma((S,))),
-        ("st_r", dma((S,))),
+        ("st_s", dma((Z,))),
+        ("st_r", dma((Z,))),
         ("p_s", dma((Z,))),
         ("p_r", dma((Z,))),
-        ("z_s", dma((Z,))),
-        ("z_r", dma((Z,))),
+        ("z_s", dma((6,))),
+        ("z_r", dma((6,))),
         ("tf_s", dma((G,))),
         ("tf_r", dma((G,))),
         ("gx_s", dma((G,))),
@@ -848,6 +985,14 @@
             flops=7 * 10**9, bytes_accessed=7 * 10**6, transcendentals=5 * 10**6
         ),
     )(*[o[1] for o in operands])
+    here = pl.BlockSpec(memory_space=pl.ANY)
+    result = pl.pallas_call(
+        functools.partial(hand_on, len(outs)),
+        out_shape=[o[1] for o in outs],
+        in_specs=[here] * len(outs),
+        out_specs=[here] * len(outs),
+        scratch_shapes=[V(o[1].shape, o[1].dtype) for o in outs] + [dma((2, len(outs)))],
+    )(*result)
     return tuple(result[:8]) + tuple(r.reshape(HD) for r in result[8:])
 
 

time: 148 us -> 121 us (0.82)
  Pallas kernels: 132 us -> 118 us
  local copies, waits for them, and re-layouts: 13.3 us -> 0.67 us
    pallas_call x1, Pallas kernels: 132 us -> 115 us  [body(): pl.pallas_call(functools.partial(kernel, S, G, names), out_shape=[o[1] fo...]
    unnamed x40 -> x2, local copies, waits for them, and re-layouts: 11.9 us -> 0.67 us
    pallas_call x0 -> x1, Pallas kernels: none -> 3.06 us  [body(): pl.pallas_call(functools.partial(hand_on, len(outs)), out_shape=[o[1] for...]
where the time goes in v2:
time: 121 us; the launch traced here: 120 us
  Pallas kernels  118 us (98%)
    pallas_call x1, Pallas kernels, body(): pl.pallas_call(functools.partial(kernel, S, G, names), out_shape=[o[1] fo...  115 us
    pallas_call x1, Pallas kernels, body(): pl.pallas_call(functools.partial(hand_on, len(outs)), out_shape=[o[1] for...  3.06 us

profile of v2, /device:TPU:1, one launch (start us, length us, event | category | flops | bytes accessed | tf_op | source)
XLA Modules:
  0.0 120.2 jit_solution(8178863266511912209)
XLA Ops:
  0.6 0.0 copy-start
  0.7 0.7 copy-done
  1.3 0.1 convert_reduce_fusion
  1.5 0.1 select_reduce_fusion
  1.6 0.5 multiply_add_fusion.refs_0_
  2.1 115.0 %shard_map.229 = (bf16[128,3072]{1,0:T(8,128)(2,1)}, bf16[8,3072]{1,0:T(8,128)(2,1)}, bf16[128,3072]{1,0:T(8,128)(2,1)}, bf16[128,3072]{1,0:T(8,128)(2,1)}, bf16...) custom-call(s32[24]{0:T(128)} %multiply_add_fusion.refs_0_, ...), custom_call_target="tpu_custom_call" | custom-call | flops 7000000000 | bytes 7000000 | tf_op jit(solution)/shard_map/pallas_call | solution.py:975
  117.1 3.1 %shard_map.230 = (bf16[128,3072]{1,0:T(8,128)(2,1)}, bf16[8,3072]{1,0:T(8,128)(2,1)}, bf16[128,3072]{1,0:T(8,128)(2,1)}, bf16[128,3072]{1,0:T(8,128)(2,1)}, bf16...) custom-call(bf16[128,3072]{1,0:T(8,128)(2,1)} %get-tuple-element.36., ...), custom_call_target="tpu_custom_call" | custom-call | tf_op jit(solution)/shard_map/pallas_call | solution.py:989
  (3 shorter events, 0.0 us)
Async XLA Ops:
  0.6 0.7 copy-start

commit v3 on v2

--- a/solution.py
+++ b/solution.py
@@ -411,7 +411,9 @@
     def forward_halo(i):
         for d in range(1, G):
             inp_in(i, d).wait_recv()
-        send_slot(i + 2)
+        if i < 2:
+            send_slot(2 * i + 2)
+            send_slot(2 * i + 3)
 
         @pl.when(s < S - 1)
         def _():
@@ -598,31 +600,29 @@
     text_out(1)
     forward_halo(1)
     text_forward(0)
-    forward_halo(2)
-    text_relay(1)
     text_in(0)
 
-    def slot_in(i):
-        for d in range(1, G):
-            inp_in(i, d).wait_recv()
-
     def attend_pair(i, carry):
+        attend(i, (3 * N + TEXT) // 256)
+
+        @pl.when(i == 0)
+        def _():
+            forward_halo(2)
+            text_relay(1)
+
         @pl.when(i == 1)
         def _():
             text_forward(1)
 
+        for d in range(1, G):
+            inp_in(LT + i, d).wait_recv()
+
         @pl.when(i == LT - 1)
         def _():
             text_in(1)
-            slot_in(L - 1)
             n.stats[0] = jnp.zeros((3, 8, TEXT), F32)
             lax.fori_loop(0, L, text_first, 0)
             stat_pair().start()
-
-        attend(i, (3 * N + TEXT) // 256)
-
-        @pl.when(i == LT - 1)
-        def _():
             stat_pair().wait_recv()
             top = jnp.maximum(n.stats[0, 0], n.stats[1, 0])
             scales = [jnp.exp2((n.stats[k, 0] - top) * SHARP) for k in range(2)]
@@ -632,23 +632,12 @@
             for d in range(1, Z):
                 stat(d).start()
 
-        @pl.when(i < LT - 1)
-        def _():
-            slot_in(LT + i)
-
-        @pl.when(i == 0)
-        def _():
-            send_slot(L - 1)
-
         attend(LT + i, (N + TEXT) // 256)
         return carry
 
     lax.fori_loop(0, LT, attend_pair, 0)
     for d in range(1, Z):
         stat_in(d).wait_recv()
-    lax.fori_loop(0, L, text_second, 0)
-    for z in range(Z):
-        pair(z).start()
 
     def finish(i, wide):
         def pack(dk, dv):
@@ -671,6 +660,7 @@
         n.orecv[1][x * L + i] = n.osend[1, i, x]
 
     def finish_flat(i, carry):
+        text_second(i, 0)
         finish(i, False)
         return carry
 
@@ -687,6 +677,9 @@
             zred(4 + k).start()
 
     lax.fori_loop(LT, L, finish_flat, 0)
+    lax.fori_loop(0, LT, text_second, 0)
+    for z in range(Z):
+        pair(z).start()
     for z in range(Z):
         pair(z).wait_recv()
         n.tz[z] = (n.tpart[2 * z + ci].astype(F32) + n.tsib[z].astype(F32)).astype(BF16)

time: 121 us -> 122 us (level)
    pallas_call x1, Pallas kernels: 115 us -> 116 us  [body(): pl.pallas_call(functools.partial(kernel, S, G, names), out_shape=[o[1] fo...]
where the time goes in v3:
time: 122 us; the launch traced here: 121 us
  Pallas kernels  119 us (98%)
    pallas_call x1, Pallas kernels, body(): pl.pallas_call(functools.partial(kernel, S, G, names), out_shape=[o[1] fo...  116 us
    pallas_call x1, Pallas kernels, body(): pl.pallas_call(functools.partial(hand_on, len(outs)), out_shape=[o[1] for...  3.06 us

profile of v3, /device:TPU:1, one launch (start us, length us, event | category | flops | bytes accessed | tf_op | source)
XLA Modules:
  0.0 121.4 jit_solution(10890658401560454267)
XLA Ops:
  0.6 0.0 copy-start
  0.7 0.7 copy-done
  1.3 0.1 convert_reduce_fusion
  1.5 0.1 select_reduce_fusion
  1.6 0.5 multiply_add_fusion.refs_0_
  2.1 116.3 %shard_map.229 = (bf16[128,3072]{1,0:T(8,128)(2,1)}, bf16[8,3072]{1,0:T(8,128)(2,1)}, bf16[128,3072]{1,0:T(8,128)(2,1)}, bf16[128,3072]{1,0:T(8,128)(2,1)}, bf16...) custom-call(s32[24]{0:T(128)} %multiply_add_fusion.refs_0_, ...), custom_call_target="tpu_custom_call" | custom-call | flops 7000000000 | bytes 7000000 | tf_op jit(solution)/shard_map/pallas_call | solution.py:968
  118.4 3.1 %shard_map.230 = (bf16[128,3072]{1,0:T(8,128)(2,1)}, bf16[8,3072]{1,0:T(8,128)(2,1)}, bf16[128,3072]{1,0:T(8,128)(2,1)}, bf16[128,3072]{1,0:T(8,128)(2,1)}, bf16...) custom-call(bf16[128,3072]{1,0:T(8,128)(2,1)} %get-tuple-element.36., ...), custom_call_target="tpu_custom_call" | custom-call | tf_op jit(solution)/shard_map/pallas_call | solution.py:982
  (3 shorter events, 0.0 us)
Async XLA Ops:
  0.6 0.7 copy-start

commit v4 on v3

--- a/solution.py
+++ b/solution.py
@@ -595,6 +595,13 @@
         n.tpart[:, 3, i] = n.dvt[i].astype(BF16).reshape(S, TS, HD)
         return carry
 
+    def text_order(p, carry):
+        h = order(p)
+        n.rawp[0, p] = n.rawt[0, h]
+        n.rawp[1, p] = n.rawt[1, h]
+        return carry
+
+    lax.fori_loop(0, HEADS, text_order, 0)
     forward_halo(0)
     text_relay(0)
     text_out(1)
@@ -744,13 +751,6 @@
 
     gain_kv = lax.fori_loop(0, HEADS // MANY, post_k, zero)
 
-    def text_order(p, carry):
-        h = order(p)
-        n.rawp[0, p] = n.rawt[0, h]
-        n.rawp[1, p] = n.rawt[1, h]
-        return carry
-
-    lax.fori_loop(0, HEADS, text_order, 0)
     for d in range(1, G):
         tfin_in(d).wait_recv()
 
@@ -972,7 +972,7 @@
         out_specs=[vmem] * len(outs),
         scratch_shapes=[o[1] for o in scratch],
         compiler_params=pltpu.CompilerParams(
-            collective_id=0, has_side_effects=True, vmem_limit_bytes=60 << 20
+            collective_id=0, has_side_effects=True, vmem_limit_bytes=50 << 20
         ),
         cost_estimate=pl.CostEstimate(
             flops=7 * 10**9, bytes_accessed=7 * 10**6, transcendentals=5 * 10**6

time: 122 us -> 130 us (1.066)
  local copies, waits for them, and re-layouts: 0.67 us -> 11.7 us
  Pallas kernels: 119 us -> 117 us
    unnamed x2 -> x44, local copies, waits for them, and re-layouts: 0.67 us -> 11.7 us
    pallas_call x1, Pallas kernels: 116 us -> 114 us  [body(): pl.pallas_call(functools.partial(kernel, S, G, names), out_shape=[o[1] fo...]
where the time goes in v4:
time: 130 us
  Pallas kernels  117 us (90%)
  local copies, waits for them, and re-layouts  11.7 us (9%)
    pallas_call x1, Pallas kernels, body(): pl.pallas_call(functools.partial(kernel, S, G, names), out_shape=[o[1] fo...  114 us
    unnamed x44, local copies, waits for them, and re-layouts  11.7 us
    pallas_call x1, Pallas kernels, body(): pl.pallas_call(functools.partial(hand_on, len(outs)), out_shape=[o[1] for...  3.05 us

profile of v4, /device:TPU:1, one launch (start us, length us, event | category | flops | bytes accessed | tf_op | source)
XLA Modules:
  0.0 130.0 jit_solution(317713045492200276)
XLA Ops:
  0.6 0.0 copy-start.21
  0.7 0.7 copy-done.21
  1.3 0.1 convert_reduce_fusion
  1.5 0.0 copy-start.18
  1.5 0.0 copy-start.19
  1.5 0.0 copy-start.20
  1.5 0.1 select_reduce_fusion
  1.6 0.0 copy-start.16
  1.6 0.0 copy-start.17
  1.7 0.5 copy-done.18
  2.1 0.0 copy-done.19
  2.2 0.0 copy-done.20
  2.2 0.1 copy-done.16
  2.3 0.0 copy-done.17
  2.3 0.0 copy-start.12
  2.3 0.8 copy-done.12
  3.1 0.0 copy-start.13
  3.1 0.8 copy-done.13
  3.9 0.0 copy-start.14
  3.9 0.8 copy-done.14
  4.7 0.0 copy-start.15
  4.7 0.8 copy-done.15
  5.5 114.2 %shard_map.229 = (bf16[128,3072]{1,0:T(8,128)(2,1)S(1)}, bf16[8,3072]{1,0:T(8,128)(2,1)S(1)}, bf16[128,3072]{1,0:T(8,128)(2,1)S(1)}, bf16[128,3072]{1,0:T(8,128)...) custom-call(s32[24]{0:T(128)S(1)} %multiply_add_fusion.refs_0_, ...), custom_call_target="tpu_custom_call" | custom-call | flops 7000000000 | bytes 7000000 | tf_op jit(solution)/shard_map/pallas_call | solution.py:968
  119.7 0.0 copy-start
  119.7 0.9 copy-done
  120.6 0.0 copy-start.1
  120.6 0.9 copy-done.1
  121.5 0.0 copy-start.2
  121.5 0.9 copy-done.2
  122.4 0.0 copy-start.3
  122.4 0.9 copy-done.3
  123.3 0.0 copy-start.4
  123.3 0.6 copy-done.4
  123.9 0.0 copy-start.5
  123.9 0.6 copy-done.5
  124.5 0.0 copy-start.6
  124.5 0.6 copy-done.6
  125.1 0.0 copy-start.7
  125.1 0.6 copy-done.7
  125.7 0.0 copy-start.11
  125.7 0.6 copy-done.11
  126.3 0.0 copy-start.8
  126.3 0.0 copy-start.9
  126.3 0.0 copy-start.10
  126.3 0.5 copy-done.8
  126.8 0.1 copy-done.9
  126.9 0.0 copy-done.10
  126.9 3.1 %shard_map.230 = (bf16[128,3072]{1,0:T(8,128)(2,1)}, bf16[8,3072]{1,0:T(8,128)(2,1)}, bf16[128,3072]{1,0:T(8,128)(2,1)}, bf16[128,3072]{1,0:T(8,128)(2,1)}, bf16...) custom-call(bf16[128,3072]{1,0:T(8,128)(2,1)} %copy-done, ...), custom_call_target="tpu_custom_call" | custom-call | tf_op jit(solution)/shard_map/pallas_call | solution.py:982
  (4 shorter events, 0.0 us)
Async XLA Ops:
  0.6 0.7 copy-start.21
  1.5 0.7 copy-start.18
  1.5 0.7 copy-start.19
  1.5 0.7 copy-start.20
  1.6 0.7 copy-start.16
  1.6 0.7 copy-start.17
  2.3 0.8 copy-start.12
  3.1 0.8 copy-start.13
  3.9 0.8 copy-start.14
  4.7 0.8 copy-start.15
  119.7 0.9 copy-start
  120.6 0.9 copy-start.1
  121.5 0.9 copy-start.2
  122.4 0.9 copy-start.3
  123.3 0.6 copy-start.4
  123.9 0.6 copy-start.5
  124.5 0.6 copy-start.6
  125.1 0.6 copy-start.7
  125.7 0.6 copy-start.11
  126.3 0.5 copy-start.8
  126.3 0.6 copy-start.9
  126.3 0.6 copy-start.10
